TPU v7x, 256 devices: a whole 4x4x8 slice. The times are simulated.
256 devices in a mesh: seq: 64 (over y, z, core), fsdp: 4 (over x).
Axes of the slice: x: 4, y: 4, z: 8, core: 2. Of those that a mesh axis runs over, the one named last changes fastest.
Arguments:
- byte_states: bfloat16 [4, 32768, 1024], P('fsdp', 'seq'), may hold values from -6 to 6
- byte_wide: bfloat16 [4, 32768, 4096], P('fsdp', 'seq'), may hold values from -6 to 6
- patch_of: int32 [4, 32768], P('fsdp', 'seq'), may hold values from 0 to 127, as said below
- w_query: bfloat16 [4096, 2048], P('fsdp'), may hold values from -0.09375 to 0.09375
- w_keyval: bfloat16 [4096, 1024], P('fsdp'), may hold values from -0.09375 to 0.09375
- w_out: bfloat16 [1024, 1024], P('fsdp'), may hold values from -0.1875 to 0.1875
- norm_gain: float32 [1024], replicated, may hold values from 0.2 to 3
- out_grad: bfloat16 [4, 32768, 1024], P('fsdp', 'seq'), may hold values from -6 to 6
Outputs:
- grad_weight: float32 [1024, 1024], P('seq')
- grad_gain: float32 [1024], replicated
Inputs may be any that keep to these rules, and one draw needn't show every extreme that they name: `patch_of`: within each shard of 512 bytes the ids start at 0 and rise by 0 or 1 from byte to byte; a shard holds from 64 to 128 patches, and in every draw some shard holds exactly 128.
All inputs are finite; a program needn't handle non-finite values.
Results may differ from a plain program's by a relative error of at most 0.02.
Values may be sent and summed in bfloat16 or wider, within the bound.
A program may use at most 128 MiB of HBM per device.

v0:
```python
import jax
import jax.numpy as jnp
from jax import lax
from jax.sharding import PartitionSpec as P

HQ = 16
HK = 4
E = 128
PCAP = 128


epsilon = 1e-05


def shifted(block, axis, distance):
    devices = range(lax.axis_size(axis))
    route = [(i - distance, i) for i in devices if i - distance in devices]
    return lax.ppermute(block, axis, route)


def on_device(byte_states, byte_wide, patch_of, w_query, w_keyval, w_out, norm_gain, out_grad):
    states = byte_states[0]
    wide_rows = byte_wide[0]
    patch_ids = patch_of[0]
    cotangent = out_grad[0]
    local_width = states.shape[1]
    group_size = HQ // HK
    dec_heads = local_width // E
    byte_count = states.shape[0]
    attn_scale = float(E) ** (-0.5)
    slot_ids = jnp.arange(PCAP, dtype=jnp.int32)
    live_count = patch_ids[-1] + 1
    shard_index = lax.axis_index("seq")
    onehot = (patch_ids[:, None] == slot_ids[None, :]).astype(jnp.bfloat16)
    pool_sums = lax.dot_general(
        onehot, wide_rows, (((0,), (0,)), ((), ())), preferred_element_type=jnp.float32
    )
    pool_sizes = jnp.sum(onehot.astype(jnp.float32), axis=0)
    pooled = (pool_sums / jnp.maximum(pool_sizes, 1.0)[:, None]).astype(jnp.bfloat16)
    pooled_f = pooled.astype(jnp.float32)
    normed = (
        pooled_f * lax.rsqrt(jnp.mean(pooled_f * pooled_f, axis=1, keepdims=True) + epsilon)
    ).astype(jnp.bfloat16)
    query_width = w_query.shape[1]
    columns = lax.all_to_all(normed, "fsdp", split_axis=1, concat_axis=0, tiled=True)
    projected = lax.psum_scatter(
        jnp.concatenate(
            [
                jnp.dot(columns, w_query, preferred_element_type=jnp.float32),
                jnp.dot(columns, w_keyval, preferred_element_type=jnp.float32),
            ],
            axis=1,
        ),
        "fsdp",
        scatter_dimension=0,
        tiled=True,
    )
    query_sum = projected[:, :query_width]
    keyval_sum = projected[:, query_width:]
    queries = query_sum.astype(jnp.bfloat16)
    keyval = keyval_sum.astype(jnp.bfloat16)
    key_rows = keyval[:, : HK * E]
    value_rows = keyval[:, HK * E :]
    live_mask = (slot_ids < live_count).astype(jnp.bfloat16)
    query_pos = shard_index * PCAP + slot_ids
    query_four = queries.reshape(PCAP, HK, group_size, E)

    def attend_block(state_in, key_piece, value_piece, live_piece, offset):
        run_max, run_total, run_acc = state_in
        span = key_piece.shape[0]
        key_pos = offset + jnp.arange(span, dtype=jnp.int32)
        allowed = (live_piece[None, :] > 0.5) & (key_pos[None, :] <= query_pos[:, None])
        scores = (
            jnp.einsum(
                "qkge,rke->kgqr",
                query_four,
                key_piece.reshape(span, HK, E),
                preferred_element_type=jnp.float32,
            ).reshape(HQ, PCAP, span)
            * attn_scale
        )
        masked = jnp.where(allowed[None], scores, -1e30)
        new_max = jnp.maximum(run_max, jnp.max(masked, axis=2))
        expo = jnp.where(allowed[None], jnp.exp(scores - new_max[..., None]), 0.0)
        decay = jnp.exp(run_max - new_max)
        new_total = run_total * decay + jnp.sum(expo, axis=2)
        mixed = jnp.einsum(
            "kgqr,rke->kgqe",
            expo.astype(jnp.bfloat16).reshape(HK, group_size, PCAP, span),
            value_piece.reshape(span, HK, E),
            preferred_element_type=jnp.float32,
        ).reshape(HQ, PCAP, E)
        return (new_max, new_total, run_acc * decay[..., None] + mixed)

    def attend(state_in, pieces, offset):
        key_piece, value_piece, live_piece = pieces
        span = key_piece.shape[0]
        block = span
        block = max((divisor for divisor in range(1, 513) if span % divisor == 0))
        if block == span:
            return attend_block(state_in, key_piece, value_piece, live_piece, offset)

        def step_block(block_index, carry):
            block_start = block_index * block
            return attend_block(
                carry,
                lax.dynamic_slice_in_dim(key_piece, block_start, block, 0),
                lax.dynamic_slice_in_dim(value_piece, block_start, block, 0),
                lax.dynamic_slice_in_dim(live_piece, block_start, block, 0),
                offset + block_start,
            )

        return lax.fori_loop(0, span // block, step_block, state_in)

    initial_state = (
        jnp.full((HQ, PCAP), -1e30, jnp.float32),
        jnp.zeros((HQ, PCAP), jnp.float32),
        jnp.zeros((HQ, PCAP, E), jnp.float32),
    )
    run_max, run_total, run_acc = attend(
        initial_state,
        (
            lax.all_gather(key_rows, "seq", axis=0, tiled=True),
            lax.all_gather(value_rows, "seq", axis=0, tiled=True),
            lax.all_gather(live_mask, "seq", axis=0, tiled=True),
        ),
        jnp.int32(0),
    )
    attended = jnp.transpose(run_acc / run_total[..., None], (1, 0, 2)).reshape(PCAP, HQ * E)
    ctx = (
        attended * lax.rsqrt(jnp.mean(attended * attended, axis=1, keepdims=True) + epsilon)
    ).astype(jnp.bfloat16)
    last_row = lax.dynamic_slice_in_dim(ctx, live_count - 1, 1, 0)
    before_row = shifted(last_row, "seq", 1)
    own_rows = jnp.dot(onehot, ctx, preferred_element_type=jnp.float32)
    prior_hot = ((patch_ids - 1)[:, None] == slot_ids[None, :]).astype(jnp.bfloat16)
    at_start = patch_ids == 0
    prior_rows = jnp.dot(prior_hot, ctx, preferred_element_type=jnp.float32)
    prior_rows = prior_rows + jnp.where(at_start[:, None], before_row.astype(jnp.float32), 0.0)
    has_prior = (patch_ids > 0) | (shard_index > 0)
    query_bytes = states.astype(jnp.float32).reshape(byte_count, dec_heads, E)
    own_key = own_rows[:, :local_width].reshape(byte_count, dec_heads, E)
    own_value = own_rows[:, local_width:].reshape(byte_count, dec_heads, E)
    prior_key = prior_rows[:, :local_width].reshape(byte_count, dec_heads, E)
    prior_value = prior_rows[:, local_width:].reshape(byte_count, dec_heads, E)
    own_score = jnp.sum(query_bytes * own_key, axis=2) * attn_scale
    prior_score = jnp.where(
        has_prior[:, None], jnp.sum(query_bytes * prior_key, axis=2) * attn_scale, -jnp.inf
    )
    pair_max = jnp.maximum(own_score, prior_score)
    own_exp = jnp.exp(own_score - pair_max)
    prior_exp = jnp.where(has_prior[:, None], jnp.exp(prior_score - pair_max), 0.0)
    attn = (own_exp[..., None] * own_value + prior_exp[..., None] * prior_value) / (
        own_exp + prior_exp
    )[..., None]
    outsum = states.astype(jnp.float32) + attn.reshape(byte_count, local_width)
    normal = outsum * lax.rsqrt(jnp.mean(outsum * outsum, axis=1, keepdims=True) + epsilon)
    decoded = (normal * norm_gain[None, :]).astype(jnp.bfloat16)
    weight_rows = lax.psum_scatter(
        lax.dot_general(
            decoded, cotangent, (((0,), (0,)), ((), ())), preferred_element_type=jnp.float32
        ),
        "seq",
        scatter_dimension=0,
        tiled=True,
    )
    back_rows = lax.dot_general(
        cotangent,
        lax.all_gather(w_out, "fsdp", axis=0, tiled=True),
        (((1,), (1,)), ((), ())),
        preferred_element_type=jnp.float32,
    )
    gain_terms = jnp.sum(back_rows * normal, axis=0)
    weight_rows = lax.psum(weight_rows, "fsdp")
    gain_sum = lax.psum(gain_terms, ("seq", "fsdp"))
    square_sum = lax.psum(jnp.sum(weight_rows * weight_rows), "seq")
    grand_total = square_sum + jnp.sum(gain_sum * gain_sum)
    clip_scale = jnp.minimum(1.0, float(local_width) / jnp.sqrt(grand_total))
    return (weight_rows * clip_scale, gain_sum * clip_scale)


def solution(mesh):
    return jax.shard_map(
        on_device,
        mesh=mesh,
        in_specs=(
            P("fsdp", "seq", None),
            P("fsdp", "seq", None),
            P("fsdp", "seq"),
            P("fsdp", None),
            P("fsdp", None),
            P("fsdp", None),
            P(),
            P("fsdp", "seq", None),
        ),
        out_specs=(P("seq", None), P()),
        check_vma=False,
    )
```

profile of v0, /device:TPU:1, one launch (start us, length us, event | category | flops | bytes accessed | tf_op | source)
XLA Modules:
  0.0 849.0 jit_solution(15981119005966969825)
XLA Ops:
  8.2 3.2 multiply_reduce_fusion.4
  11.8 19.0 %all_to_all.19 = bf16[128,4,1024]{2,0,1:T(8,128)(2,1)S(1)} all-to-all(bf16[128,4,1024]{2,0,1:T(8,128)(2,1)S(1)} %bitcast.138), channel_id=1, replica_groups=mesh['seq'=64,'fsdp'=4] {'fsdp'}, dimensions={1} | all-to-all | bytes 2097152 | tf_op jit(solution)/shard_map/all_to_all | solution.py:45
  30.8 2.4 fusion.43
  34.4 3.1 pad_maximum_fusion
  37.6 69.0 %reduce-scatter.3.cloned.1.call-done = f32[128,3072]{1,0:T(8,128)} async-done(((f32[512,3072]{1,0:T(8,128)}), f32[128,3072]{1,0:T(8,128)}) %reduce-scatter.3.cloned.1.call-update) | async-done | bytes 1572880 | tf_op jit(solution)/shard_map/reduce_scatter | solution.py:46
  106.6 1.5 convert.7
  112.3 1.5 convert_bitcast_fusion
  113.7 1.8 copy.54
  115.5 41.8 %all-gather = bf16[64,1,128]{2,1,0:T(2,128)(2,1)S(1)} all-gather(bf16[1,1,128]{2,1,0:T(2,128)(2,1)S(1)} %fusion.37), channel_id=1, replica_groups=mesh['seq'=64,'fsdp'=4] {'seq'}, dimensions={0}, use_global_device_ids=true | all-gather | bytes 16640 | tf_op jit(solution)/shard_map/all_gather | solution.py:125
  159.7 32.9 %all-gather.5.cloned.1.call-done = bf16[8192,512]{1,0:T(8,128)(2,1)} async-done(((bf16[128,512]{1,0:T(8,128)(2,1)}), bf16[8192,512]{1,0:T(8,128)(2,1)}) %all-gather.5.cloned.1.call-update) | async-done | bytes 8388624 | tf_op jit(solution)/shard_map/all_gather | solution.py:123
  192.6 83.1 %all-gather.7.cloned.1.call-done = bf16[8192,512]{1,0:T(8,128)(2,1)} async-done(((bf16[128,512]{1,0:T(8,128)(2,1)}), bf16[8192,512]{1,0:T(8,128)(2,1)}) %all-gather.7.cloned.1.call-update) | async-done | bytes 8388624 | tf_op jit(solution)/shard_map/all_gather | solution.py:124
  275.8 158.1 %while.18 = (s32[]{:T(128)}, f32[16,128]{1,0:T(8,128)S(1)}, f32[16,128]{1,0:T(8,128)S(1)}, f32[16,128,128]{2,1,0:T(8,128)S(1)}, bf16[8192]{0:T(1024)(128)(2,1)S(...) while((s32[]{:T(128)}, f32[16,128]{1,0:T(8,128)S(1)}, ...), condition=%wide.region_6.7_spmd.clone, body=%wide.region_3.6_spmd.clone.sunk | while | flops 549335168 | bytes 39722208 | solution.py:113
  276.1 1.3 constant_dynamic-slice_fusion.4
  277.6 2.8 fusion.67
  280.6 3.6 fusion.70
  287.4 2.8 fusion.67
  290.4 3.6 fusion.70
  295.8 1.3 constant_dynamic-slice_fusion.4
  297.3 2.8 fusion.67
  300.3 3.6 fusion.70
  307.2 2.8 fusion.67
  310.2 3.6 fusion.70
  315.6 1.3 constant_dynamic-slice_fusion.4
  317.1 2.8 fusion.67
  320.1 3.6 fusion.70
  325.5 1.3 constant_dynamic-slice_fusion.4
  327.0 2.8 fusion.67
  330.0 3.6 fusion.70
  335.3 1.3 constant_dynamic-slice_fusion.4
  336.8 2.8 fusion.67
  339.8 3.6 fusion.70
  345.2 1.3 constant_dynamic-slice_fusion.4
  346.7 2.8 fusion.67
  349.7 3.6 fusion.70
  355.1 1.3 constant_dynamic-slice_fusion.4
  356.6 2.8 fusion.67
  359.6 3.6 fusion.70
  365.0 1.3 constant_dynamic-slice_fusion.4
  366.5 2.8 fusion.67
  369.5 3.6 fusion.70
  374.9 1.3 constant_dynamic-slice_fusion.4
  376.4 2.8 fusion.67
  379.4 3.6 fusion.70
  386.2 2.8 fusion.67
  389.2 3.6 fusion.70
  396.1 2.8 fusion.67
  399.1 3.6 fusion.70
  406.0 2.8 fusion.67
  409.0 3.6 fusion.70
  415.9 2.8 fusion.67
  418.9 3.6 fusion.70
  425.8 2.8 fusion.67
  428.8 3.6 fusion.70
  435.5 3.7 collective-permute-start
  439.8 5.3 collective-permute-done
  451.0 1.7 multiply_reduce_fusion.1
  452.8 3.3 fusion.21
  456.8 137.0 %reduce-scatter.5.cloned.1.call-done = f32[16,1024]{1,0:T(8,128)} async-done(((f32[1024,1024]{1,0:T(8,128)}), f32[16,1024]{1,0:T(8,128)}) %reduce-scatter.5.cloned.1.call-update) | async-done | bytes 65552 | tf_op jit(solution)/shard_map/reduce_scatter | solution.py:159
  593.8 38.5 %all-gather.9.cloned.1.call-done = bf16[1024,1024]{1,0:T(8,128)(2,1)} async-done(((bf16[256,1024]{1,0:T(8,128)(2,1)}), bf16[1024,1024]{1,0:T(8,128)(2,1)}) %all-gather.9.cloned.1.call-update) | async-done | bytes 2097168 | tf_op jit(solution)/shard_map/all_gather | solution.py:169
  632.2 3.5 multiply_reduce_fusion
  635.8 76.2 %psum.23 = f32[1024]{0:T(1024)S(1)} all-reduce(f32[1024]{0:T(1024)S(1)} %multiply_reduce_fusion), channel_id=1, replica_groups=mesh['seq'=64,'fsdp'=4] {'seq','fsdp'}, use_global_device_ids=true, to_apply=%region_16.17 | all-reduce | flops 1024 | bytes 8192 | tf_op jit(solution)/shard_map/psum | solution.py:175
  712.0 1.5 multiply_reduce_fusion.5
  714.0 124.7 %psum.22 = f32[]{:T(128)} all-reduce(f32[]{:T(128)} %multiply_reduce_fusion.5), channel_id=1, replica_groups=mesh['seq'=64,'fsdp'=4] {'seq'}, use_global_device_ids=true, to_apply=%region_14.15 | all-reduce | flops 1 | bytes 8 | tf_op jit(solution)/shard_map/psum | solution.py:176
  840.7 1.5 broadcast_multiply_fusion
  (286 shorter events, 60.2 us)
Async XLA Ops:
  7.2 26.0 %copy-start = (bf16[1024,1024]{1,0:T(8,128)(2,1)S(1)}, bf16[1024,1024]{1,0:T(8,128)(2,1)}, u32[]{:S(2)}) copy-start(bf16[1024,1024]{1,0:T(8,128)(2,1)} %param.14) | copy-start | bytes 6291460
  7.2 99.4 %reduce-scatter.3.cloned.1.call-start = ((), (), s32[]{:S(2)}) async-start(), calls=%async_computation.3 | async-start | bytes 7864320 | tf_op jit(solution)/shard_map/reduce_scatter | solution.py:46
  11.7 19.1 %copy-start.10 = (bf16[1024,2048]{1,0:T(8,128)(2,1)S(1)}, bf16[1024,2048]{1,0:T(8,128)(2,1)}, u32[]{:S(2)}) copy-start(bf16[1024,2048]{1,0:T(8,128)(2,1)} %param.13) | copy-start | bytes 12582916
  37.5 72.2 %copy-start.9 = (s32[1,512]{1,0:T(1,128)S(1)}, s32[1,512]{1,0:T(1,128)}, u32[]{:S(2)}) copy-start(s32[1,512]{1,0:T(1,128)} %param.12) | copy-start | bytes 6148
  37.5 155.1 %all-gather.5.cloned.1.call-start = ((), (), s32[]{:S(2)}) async-start(), calls=%async_computation.4 | async-start | bytes 8519680 | tf_op jit(solution)/shard_map/all_gather | solution.py:123
  108.1 3.5 copy-start.6
  108.9 166.9 %all-gather.7.cloned.1.call-start = ((), (), s32[]{:S(2)}) async-start(), calls=%async_computation.5 | async-start | bytes 8519680 | tf_op jit(solution)/shard_map/all_gather | solution.py:124
  109.7 484.1 %reduce-scatter.5.cloned.1.call-start = ((), (), s32[]{:S(2)}) async-start(), calls=%async_computation.6 | async-start | bytes 4259840 | tf_op jit(solution)/shard_map/reduce_scatter | solution.py:159
  280.6 3.6 copy-start.2
  290.4 3.6 copy-start.2
  300.3 3.6 copy-start.2
  310.2 3.6 copy-start.2
  320.1 3.6 copy-start.2
  329.9 3.6 copy-start.2
  339.8 3.6 copy-start.2
  349.7 3.6 copy-start.2
  359.6 3.6 copy-start.2
  369.5 3.6 copy-start.2
  379.3 3.6 copy-start.2
  389.2 3.6 copy-start.2
  399.1 3.6 copy-start.2
  409.0 3.6 copy-start.2
  418.9 3.6 copy-start.2
  428.7 3.6 copy-start.2
  435.5 9.6 %collective-permute-start = (bf16[1,2048]{0,1:T(8,128)(2,1)S(1)}, bf16[1,2048]{0,1:T(8,128)(2,1)S(1)}, u32[]{:S(2)}, u32[]{:S(2)}) collective-permute-start(bf16[1,2048]{0,1:T(8,128)(2,1)S(1)} %constant_dynamic-slice_fusion.2), channel_id=1, source_target_pairs={{0,4},{4,8},{8,12},{12,16},{16,20},{20,24},{24,28},{28,32},{32,36}... | collective-permute-start | bytes 12296 | tf_op jit(solution)/shard_map/ppermute | solution.py:18
  446.2 1.6 copy-start.4
  449.8 1.2 copy-start.5
  451.0 1.8 copy-start.7
  451.0 1.8 copy-start.8
  452.8 3.4 copy-start.3
  456.2 176.1 %all-gather.9.cloned.1.call-start = ((), (), s32[]{:S(2)}) async-start(), calls=%async_computation.8 | async-start | bytes 2621440 | tf_op jit(solution)/shard_map/all_gather | solution.py:169
  456.7 255.2 %all-reduce.2.cloned.1.call-start = ((), (), s32[]{:S(2)}) async-start(), calls=%async_computation.7 | async-start | bytes 131072 | tf_op jit(solution)/shard_map/psum | solution.py:174
  593.8 248.4 %copy-start.1 = (bf16[1024,1024]{1,0:T(8,128)(2,1)S(1)}, bf16[1024,1024]{1,0:T(8,128)(2,1)}, u32[]{:S(2)}) copy-start(bf16[1024,1024]{1,0:T(8,128)(2,1)} %param.14) | copy-start | bytes 6291460
Sparse Core Ops, SparseCore 0:
  37.6 68.9 reduce-scatter.2
  109.4 83.2 all-gather.4
  195.4 80.3 all-gather.6
  456.3 137.4 reduce-scatter.4
  595.6 36.6 all-gather.8
  634.5 43.9 all-reduce.1
where the time goes:
time: 850 us; the launch traced here: 849 us
  waiting for transfers between devices  367 us (43%)
  blocking collectives  262 us (31%)
  matrix products  117 us (14%)
  other arithmetic  43 us (5%)
  local copies, waits for them, and re-layouts  36.9 us (4%)
  between operations  18.4 us (2%)
    reduce_scatter x1, waiting for transfers between devices, on_device(): lax.psum_scatter(lax.dot_general(decoded, cotangent, (((0,), (0,)), ((),...  137 us
    psum x1, blocking collectives, on_device(): square_sum = lax.psum(jnp.sum(weight_rows * weight_rows), 'seq')  125 us
    all_gather x1, waiting for transfers between devices, on_device(): lax.all_gather(value_rows, 'seq', axis=0, tiled=True)  83.1 us
    psum x1, blocking collectives, on_device(): gain_sum = lax.psum(gain_terms, ('seq', 'fsdp'))  76.2 us
    reduce_scatter x1, waiting for transfers between devices, on_device(): lax.psum_scatter(jnp.concatenate([jnp.dot(columns, w_query, preferred_ele...  69 us
    dot_general x16, matrix products, attend_block(): jnp.einsum('kgqr,rke->kgqe', expo.astype(jnp.bfloat16).reshape(HK, group_...  57.4 us
    dot_general x16, matrix products, attend_block(): jnp.einsum('qkge,rke->kgqr', query_four, key_piece.reshape(span, HK, E),...  44.2 us
    all_gather x1, blocking collectives, on_device(): lax.all_gather(live_mask, 'seq', axis=0, tiled=True)  41.8 us
  transfers between devices with their start and end apart: 7, of which 6 were waited for; matrix products, arithmetic and copies ran while one was open for 1% of the time, Pallas kernels for 0%

commit v1 on v0

v1 whole, which is shorter than its diff:
```python
import jax
import jax.numpy as jnp
from jax import lax
from jax.experimental import pallas as pl
from jax.experimental.pallas import tpu as pltpu
from jax.sharding import PartitionSpec as P

E = 128
PCAP = 128
NY, NZ, NX = 4, 8, 4
EPS = 1e-05
DEAD_ROW = 1024.0
DEAD_KEY = 4096.0
NEG = -1e30
Q_SCALE = float(E) ** (-0.5) * 1.4426950408889634
MESH = pl.DeviceIdType.MESH
F32 = jnp.float32
BF16 = jnp.bfloat16


def place():
    seq = lax.axis_index("seq")
    return seq // 16, (seq // 2) % 8, seq % 2, lax.axis_index("fsdp")


def dev(y, z, c, x):
    return {"seq": (y * 8 + z) * 2 + c, "fsdp": x}


def greet(peers):
    barrier = pltpu.get_barrier_semaphore()
    for peer in peers:
        pl.semaphore_signal(barrier, inc=1, device_id=peer, device_id_type=MESH)
    pl.semaphore_wait(barrier, len(peers))


def remote(src, dst, send, recv, peer):
    return pltpu.make_async_remote_copy(
        src_ref=src, dst_ref=dst, send_sem=send, recv_sem=recv, device_id=peer, device_id_type=MESH
    )


def dot(a, b, ca=1, cb=0):
    return lax.dot_general(a, b, (((ca,), (cb,)), ((), ())), preferred_element_type=F32)


def iota(shape, axis):
    return lax.broadcasted_iota(jnp.int32, shape, axis)


def project_kernel(ids_ref, wide_ref, wq_ref, wkv_ref, q_ref, kv_ref,
                   wide_v, pooled, nrm, wbuf, acc, lsem, ysend, yrecv, xsend, xrecv, ssend, srecv):
    y, z, c, x = place()
    right, left = dev((y + 1) % 4, z, c, x), dev((y + 3) % 4, z, c, x)
    xright, xleft = dev(y, z, c, (x + 1) % 4), dev(y, z, c, (x + 3) % 4)
    sibling = dev(y, z, 1 - c, x)

    loads = [
        pltpu.make_async_copy(wq_ref.at[:, pl.ds(pl.multiple_of(512 * y, 128), 512)], wbuf.at[0, :, pl.ds(0, 512)], lsem.at[0]),
        pltpu.make_async_copy(wkv_ref.at[:, pl.ds(pl.multiple_of(128 * y, 128), 128)], wbuf.at[0, :, pl.ds(512, 128)], lsem.at[1]),
        pltpu.make_async_copy(wkv_ref.at[:, pl.ds(pl.multiple_of(512 + 128 * y, 128), 128)], wbuf.at[0, :, pl.ds(640, 128)], lsem.at[2]),
    ] + [
        pltpu.make_async_copy(wide_ref.at[:, pl.ds(1024 * k, 1024)], wide_v.at[k], lsem.at[3 + k]) for k in range(4)
    ]
    for load in loads:
        load.start()
    greet([right, left, xright, xleft, sibling])

    def part(slot, owner, half):
        return wbuf.at[slot, pl.ds(pl.multiple_of(512 * owner + 256 * half, 256), 256)]

    for load in loads[:3]:
        load.wait()
    wsends = []
    for direction, peer in ((0, xright), (1, xleft)):
        for half in ((0, 1) if direction == 0 else (1, 0)):
            copy = remote(part(0, c, half), part(1 + direction, c, half),
                          xsend.at[2 * direction + half], xrecv.at[2 * direction + half], peer)
            copy.start()
            wsends.append(copy)

    onehot = (iota((PCAP, 512), 0) == ids_ref[...]).astype(F32)
    sizes = jnp.sum(onehot, axis=1, keepdims=True)
    onehot = onehot.astype(BF16)
    inverse = 1.0 / jnp.maximum(sizes, 1.0)
    squares = jnp.zeros((PCAP, 1), F32)
    for k in range(4):
        loads[3 + k].wait()
        chunk = (dot(onehot, wide_v[k]) * inverse).astype(BF16)
        pooled[k] = chunk
        chunk = chunk.astype(F32)
        squares = squares + jnp.sum(chunk * chunk, axis=1, keepdims=True)
    scale = lax.rsqrt(squares / 4096.0 + EPS)
    for k in range(4):
        chunk = pooled[k].astype(F32) * scale
        if k == 0:
            chunk = jnp.where((iota((PCAP, 1024), 1) == 0) & (sizes < 0.5), DEAD_ROW, chunk)
        nrm[k, 0] = chunk.astype(BF16)

    rows = []
    for first, second in ((0, 3), (1, 2), (2, 1), (3, 0)):
        for direction, peer, k in ((0, right, first), (1, left, second)):
            copy = remote(nrm.at[k, 0], nrm.at[k, 1 + direction],
                          ysend.at[direction, k], yrecv.at[direction, k], peer)
            copy.start()
            rows.append((direction, k, copy))
    arrivals = {(direction, k): copy for direction, k, copy in rows}
    warrivals = {(0, 0): wsends[0], (0, 1): wsends[1], (1, 1): wsends[2], (1, 0): wsends[3]}

    ysends = [copy for _, _, copy in rows]
    lasts, wlasts, ssends = [], [], []

    def give(slot, half):
        i = 2 * (slot - 1) + half
        copy = remote(part(slot, c, half), part(slot, c, half), ssend.at[i], srecv.at[i], sibling)
        copy.start()
        ssends.append(copy)

    def pass_rows(direction, k, peer):
        arrivals[direction, k].wait_recv()
        copy = remote(nrm.at[k, 1 + direction], nrm.at[k, 3], ysend.at[2, k], yrecv.at[2, k], peer)
        copy.start()
        lasts.append(copy)

    def pass_weights(direction, half, peer):
        warrivals[direction, half].wait_recv()
        if peer is not None:
            copy = remote(part(1 + direction, c, half), part(3, c, half), xsend.at[4 + half], xrecv.at[4 + half], peer)
            copy.start()
            wlasts.append(copy)
        give(1 + direction, half)

    pass_weights(0, 0, xright)
    pass_weights(1, 1, xleft)
    pass_rows(0, 0, right)
    pass_rows(1, 3, left)
    pass_rows(0, 1, right)
    pass_rows(1, 2, left)
    pass_weights(0, 1, None)
    pass_weights(1, 0, None)
    for half, copy in enumerate(wlasts):
        copy.wait_recv()
        give(3, half)
    for direction, k in ((0, 2), (1, 1), (0, 3), (1, 0)):
        arrivals[direction, k].wait_recv()
    for slot in (1, 2, 3):
        for half in range(2):
            i = 2 * (slot - 1) + half
            remote(part(slot, 1 - c, half), part(slot, 1 - c, half), ssend.at[i], srecv.at[i], sibling).wait_recv()

    for at, step in enumerate((0, 3, 1, 2)):
        k = (x + step) % 4
        value = dot(nrm[k, 0:3].reshape(384, 1024), wbuf[at])
        if at == 0:
            acc[0:384] = value
        else:
            acc[0:384] += value
    for copy in lasts:
        copy.wait_recv()
    for at, step in enumerate((0, 3, 1, 2)):
        k = (x + step) % 4
        value = dot(nrm[k, 3], wbuf[at])
        if at == 0:
            acc[384:512] = value
        else:
            acc[384:512] += value

    ones = (iota((512, 128), 1) == 0).astype(F32).astype(BF16)
    for slot, step in enumerate((0, 3, 1, 2)):
        at = (y + step) % 4
        here = pl.ds(128 * slot, 128)
        for g in range(4):
            q_ref[at, pl.ds(128 * g, 128), pl.ds(0, 128)] = (acc[here, pl.ds(128 * g, 128)] * Q_SCALE).astype(BF16)
        q_ref[at, :, pl.ds(128, 128)] = ones
        dead = nrm[0, slot][:, 0:128].astype(F32)[:, 0:1] > 512.0
        kv_ref[0, at] = jnp.where(dead, DEAD_KEY, acc[here, pl.ds(512, 128)]).astype(BF16)
        kv_ref[1, at] = acc[here, pl.ds(640, 128)].T.astype(BF16)

    for copy in wsends + wlasts + ysends + lasts + ssends:
        copy.wait_send()


def attend_kernel(ids_ref, q_ref, kv_ref, ctx_ref,
                  blocks, kext, top, total, acc, osend, att, row_out, row_in,
                  zsend, ssend, recv, asend, arecv, rsend, rrecv):
    y, z, c, x = place()
    seq = lax.axis_index("seq")
    sibling = dev(y, z, 1 - c, x)
    dirn = 1 - 2 * c
    za, zb = dev(y, (z + dirn + 8) % 8, c, x), dev(y, (z - dirn + 8) % 8, c, x)
    mates = [dev((y + d) % 4, z, c, x) for d in (1, 2, 3)]
    following = {"seq": (seq + 1) % 64, "fsdp": x}
    before_me = {"seq": (seq + 63) % 64, "fsdp": x}

    blocks[0] = kv_ref[...]
    greet([za, zb, sibling] + mates + [following, before_me])

    first = [
        remote(blocks.at[0], blocks.at[1], zsend.at[1], recv.at[1], za),
        remote(blocks.at[0], blocks.at[2], zsend.at[2], recv.at[2], zb),
        remote(blocks.at[0], blocks.at[8], ssend.at[0], recv.at[8], sibling),
    ]
    for copy in first:
        copy.start()

    def load_keys(slot):
        keys = blocks[slot, 0].reshape(512, 128)
        kext[:, 0:128] = keys
        dead = keys.astype(F32)[:, 0:1] > 2000.0
        kext[:, 128:256] = jnp.broadcast_to(jnp.where(dead, NEG, 0.0), (512, 128)).astype(BF16)

    def update(slot, yq, count, fresh):
        scores = dot(kext[0:128 * count], q_ref[yq], 1, 1)
        if fresh:
            last = scores[128 * (count - 1):]
            allowed = iota((128, 512), 0) <= iota((128, 512), 1) % 128
            last = jnp.where(allowed, last, NEG)
            scores = jnp.concatenate([scores[: 128 * (count - 1)], last], axis=0) if count > 1 else last
        peak = jnp.max(scores, axis=0, keepdims=True)
        if not fresh:
            old = top[yq]
            peak = jnp.maximum(peak, old)
            decay = jnp.exp2(old - peak)
        probs = jnp.exp2(scores - peak)
        sums = jnp.sum(probs, axis=0, keepdims=True)
        values = jnp.concatenate([blocks[slot, 1, i] for i in range(count)], axis=1)
        mixed = dot(values, probs.astype(BF16))
        top[yq] = peak
        if fresh:
            total[yq] = sums
            acc[yq] = mixed
        else:
            total[yq] = total[yq] * decay + sums
            acc[yq] = acc[yq] * decay + mixed

    load_keys(0)
    for yq in range(4):
        update(0, yq, yq + 1, True)

    def item(i, carry):
        s = (i + 1) // 2
        sib = (i + 1) % 2
        slot = s + 8 * sib
        hop = (s + 1) // 2
        odd = s % 2
        remote(blocks.at[slot], blocks.at[slot], zsend.at[1], recv.at[slot], sibling).wait_recv()

        @pl.when((sib == 0) & (s <= 5))
        def _():
            step = dirn * (2 * odd - 1)
            remote(blocks.at[s], blocks.at[s + 2], zsend.at[s + 2], recv.at[s + 2],
                   dev(y, (z + step + 8) % 8, c, x)).start()

        @pl.when(sib == 0)
        def _():
            remote(blocks.at[s], blocks.at[8 + s], ssend.at[s], recv.at[8 + s], sibling).start()

        back = hop * dirn * (1 - 2 * sib) * (2 * odd - 1)
        zsrc = (z - back + 8) % 8
        csrc = (1 - sib) * c + sib * (1 - c)
        earlier = 2 * zsrc + csrc < 2 * z + c
        load_keys(slot)

        @pl.when(earlier)
        def _():
            for yq in range(4):
                update(slot, yq, yq + 1, False)

        @pl.when(jnp.logical_not(earlier))
        def _():
            for yq in range(1, 4):
                update(slot, yq, yq, False)

        return carry

    lax.fori_loop(0, 15, item, 0)

    for yq in range(4):
        out = acc[yq] / total[yq]
        for g in range(4):
            osend[yq, :, pl.ds(128 * g, 128)] = out[:, 128 * g:128 * g + 128].T.astype(BF16)
    sends = []
    for d in (1, 2, 3):
        copy = remote(osend.at[(y + d) % 4], att.at[y], asend.at[d], arecv.at[d], mates[d - 1])
        copy.start()
        sends.append(copy)
    att[y] = osend[y]
    for d, copy in zip((1, 2, 3), sends):
        remote(att.at[(y + 4 - d) % 4], att.at[(y + 4 - d) % 4], asend.at[d], arecv.at[d], mates[d - 1]).wait_recv()

    squares = jnp.zeros((PCAP, 1), F32)
    for h in range(4):
        part = att[h].astype(F32)
        squares = squares + jnp.sum(part * part, axis=1, keepdims=True)
    scale = lax.rsqrt(squares / 2048.0 + EPS)
    final = jnp.max(ids_ref[...].astype(F32), axis=1, keepdims=True).astype(jnp.int32)
    pick = (iota((16, PCAP), 1) == final).astype(F32).astype(BF16)
    for h in range(4):
        ctx = (att[h].astype(F32) * scale).astype(BF16)
        ctx_ref[h, 0:128] = ctx
        row_out[h] = dot(pick, ctx).astype(BF16)
    copy = remote(row_out, row_in, rsend, rrecv, following)
    copy.start()
    copy.wait()
    for h in range(4):
        ctx_ref[h, 128:144] = row_in[h]

    for copy in first + sends:
        copy.wait_send()

    def drain(s, carry):
        remote(blocks.at[s], blocks.at[s], zsend.at[s], recv.at[s], sibling).wait_send()
        return carry

    lax.fori_loop(3, 8, drain, 0)

    def drain_sibling(s, carry):
        remote(blocks.at[s], blocks.at[s], ssend.at[s], recv.at[s], sibling).wait_send()
        return carry

    lax.fori_loop(1, 8, drain_sibling, 0)


def grad_kernel(ids_ref, states_ref, ctx_ref, gain_ref, grad_ref, wout_ref, out_ref, gout_ref,
                sums_t, dec, sib_out, sib_in, y1_out, y2_out, y1_in, y2_in, z_out, z_in, xs, wrow, t1, t2,
                ssend, srecv, ysend, yrecv, zsend, zrecv, xsend, xrecv, wsend, wrecv, asend, arecv, bsend, brecv):
    y, z, c, x = place()
    seq = lax.axis_index("seq")
    me = 2 * z + c
    sibling = dev(y, z, 1 - c, x)
    right, left = dev((y + 1) % 4, z, c, x), dev((y + 3) % 4, z, c, x)
    ymates = [dev((y + d) % 4, z, c, x) for d in (1, 2, 3)]
    xmates = [dev(y, z, c, (x + d) % 4) for d in (1, 2, 3)]
    pmates = [{"seq": 16 * y + (me + d) % 16, "fsdp": x} for d in range(1, 16)]
    greet(ymates + xmates + pmates)

    wcopies = [remote(wout_ref.at[pl.ds(pl.multiple_of(16 * me, 16), 16)], wrow, wsend.at[d], wrecv, xmates[d]) for d in range(3)]

    @pl.when(x == y)
    def _():
        for copy in wcopies:
            copy.start()

    ids = ids_ref[...]
    own_hot = iota((144, 512), 0) == ids
    prior_hot = iota((144, 512), 0) == jnp.where(ids > 0, ids - 1, 128)
    has_prior = (ids > 0) | (seq > 0)
    squares = jnp.zeros((1, 512), F32)
    for h in range(8):
        lanes = pl.ds(128 * (h % 4), 128)
        states = states_ref[:, pl.ds(128 * h, 128)].astype(F32).T
        keys = ctx_ref[h // 4, :, lanes]
        values = ctx_ref[2 + h // 4, :, lanes]
        scores = dot(keys, states.astype(BF16)) * Q_SCALE
        own = jnp.sum(jnp.where(own_hot, scores, 0.0), axis=0, keepdims=True)
        prior = jnp.sum(jnp.where(prior_hot, scores, 0.0), axis=0, keepdims=True)
        prior = jnp.where(has_prior, prior, NEG)
        peak = jnp.maximum(own, prior)
        own = jnp.exp2(own - peak)
        prior = jnp.exp2(prior - peak)
        scale = 1.0 / (own + prior)
        weights = jnp.where(own_hot, own * scale, jnp.where(prior_hot, prior * scale, 0.0))
        attn = dot(values, weights.astype(BF16), 0, 0)
        total = states + attn
        squares = squares + jnp.sum(total * total, axis=0, keepdims=True)
        sums_t[pl.ds(128 * h, 128)] = total
    scale = lax.rsqrt(squares / 1024.0 + EPS)
    for h in range(8):
        gain = jnp.broadcast_to(gain_ref[h:h + 1], (128, 128)).T[:, 0:1]
        rows = ((sums_t[pl.ds(128 * h, 128)] * scale) * gain).astype(BF16)
        for i in range(8):
            at = (h % 2) * 4 + i // 2
            dec[i % 2, h // 2, pl.ds(16 * at, 16)] = rows[16 * i:16 * i + 16]

    order = [(y + 2) % 4, (y + 1) % 4, (y + 3) % 4, y]
    sib_copies = []
    for i, at in enumerate(order):
        sib_out[i] = dot(dec[1 - c, at], grad_ref[...]).astype(BF16)
        copy = remote(sib_out.at[i], sib_in.at[i], ssend.at[i], srecv.at[i], sibling)
        copy.start()
        sib_copies.append(copy)

    def chunk(i):
        mine = dot(dec[c, order[i]], grad_ref[...])
        sib_copies[i].wait_recv()
        return mine + sib_in[i].astype(F32)

    far = chunk(0)
    y1_out[0] = far[:, :512].astype(BF16)
    y1_out[1] = far[:, 512:].astype(BF16)
    ones = [remote(y1_out.at[0], y1_in.at[0], ysend.at[0], yrecv.at[0], right),
            remote(y1_out.at[1], y1_in.at[1], ysend.at[1], yrecv.at[1], left)]
    for copy in ones:
        copy.start()
    to_right = chunk(1)
    to_left = chunk(2)
    ones[0].wait_recv()
    y2_out[0, :, 0:512] = (to_right[:, :512] + y1_in[0].astype(F32)).astype(BF16)
    y2_out[0, :, 512:1024] = to_right[:, 512:].astype(BF16)
    twos = [remote(y2_out.at[0], y2_in.at[0], ysend.at[2], yrecv.at[2], right),
            remote(y2_out.at[1], y2_in.at[1], ysend.at[3], yrecv.at[3], left)]
    twos[0].start()
    ones[1].wait_recv()
    y2_out[1, :, 0:512] = to_left[:, :512].astype(BF16)
    y2_out[1, :, 512:1024] = (to_left[:, 512:] + y1_in[1].astype(F32)).astype(BF16)
    twos[1].start()
    mine = chunk(3)
    for copy in twos:
        copy.wait_recv()
    mine = mine + y2_in[0].astype(F32) + y2_in[1].astype(F32)
    z_out[...] = mine.astype(BF16).reshape(8, 16, 1024)
    z_copies = []
    for d in range(1, 8):
        copy = remote(z_out.at[(z + d) % 8], z_in.at[d], zsend.at[d], zrecv.at[d], dev(y, (z + d) % 8, c, x))
        copy.start()
        z_copies.append(copy)
    rows = z_out[z].astype(F32)
    for d in range(1, 8):
        z_copies[d - 1].wait_recv()
        rows = rows + z_in[d].astype(F32)
    xs[x] = rows
    x_copies = []
    for d in (1, 2, 3):
        copy = remote(xs.at[x], xs.at[x], xsend.at[d], xrecv.at[d], xmates[d - 1])
        copy.start()
        x_copies.append(copy)

    @pl.when(x == y)
    def _():
        wrow[...] = wout_ref[pl.ds(pl.multiple_of(16 * me, 16), 16)]

    @pl.when(x != y)
    def _():
        wcopies[0].wait_recv()

    for d in (1, 2, 3):
        remote(xs.at[(x + 4 - d) % 4], xs.at[(x + 4 - d) % 4], xsend.at[d], xrecv.at[d], xmates[d - 1]).wait_recv()
    rows = (xs[0] + xs[1]) + (xs[2] + xs[3])

    gains = jnp.sum(rows * wrow[...].astype(F32), axis=1, keepdims=True)
    lane = (z % 4) * 32 + c * 16
    spread = jnp.where(iota((16, 128), 1) == iota((16, 128), 0) + lane, gains, 0.0)
    spread = jnp.sum(spread, axis=0, keepdims=True)
    power = jnp.sum(rows * rows, axis=0, keepdims=True)
    parts = power[:, 0:128]
    for i in range(1, 8):
        parts = parts + power[:, 128 * i:128 * i + 128]
    row = iota((8, 128), 0)
    upper = jnp.where(row == 2 * y + z // 4, spread, 0.0) / gain_ref[...]
    t1[me, 0:8] = upper
    t1[me, 8:16] = jnp.where(row == 0, parts, 0.0)
    a_copies = []
    for d in range(1, 16):
        copy = remote(t1.at[me], t1.at[me], asend.at[d], arecv.at[d], pmates[d - 1])
        copy.start()
        a_copies.append(copy)
    for d in range(1, 16):
        there = (me + 16 - d) % 16
        remote(t1.at[there], t1.at[there], asend.at[d], arecv.at[d], pmates[d - 1]).wait_recv()
    tile = t1[0]
    for i in range(1, 16):
        tile = tile + t1[i]
    t2[y] = tile
    b_copies = []
    for d in (1, 2, 3):
        copy = remote(t2.at[y], t2.at[y], bsend.at[d], brecv.at[d], ymates[d - 1])
        copy.start()
        b_copies.append(copy)
    for d in (1, 2, 3):
        there = (y + 4 - d) % 4
        remote(t2.at[there], t2.at[there], bsend.at[d], brecv.at[d], ymates[d - 1]).wait_recv()
    tile = (t2[0] + t2[1]) + (t2[2] + t2[3])
    gsum = tile[0:8]
    grand = jnp.sum(tile[8:16] + gsum * gsum, axis=0, keepdims=True)
    grand = jnp.sum(grand, axis=1, keepdims=True)
    clip = jnp.minimum(1.0, 1024.0 / jnp.sqrt(grand))
    out_ref[...] = rows * clip
    gout_ref[...] = gsum * clip

    for copy in sib_copies + ones + twos + z_copies + x_copies + a_copies + b_copies:
        copy.wait_send()

    @pl.when(x == y)
    def _():
        for copy in wcopies:
            copy.wait_send()


VMEM = pl.BlockSpec(memory_space=pltpu.VMEM)
ANY = pl.BlockSpec(memory_space=pl.ANY)
DMA = pltpu.SemaphoreType.DMA


def params(number):
    return pltpu.CompilerParams(collective_id=number, has_side_effects=True, vmem_limit_bytes=56 * 1024 * 1024)


def project(ids, wide, wq, wkv):
    return pl.pallas_call(
        project_kernel,
        out_shape=[jax.ShapeDtypeStruct((4, 512, 256), BF16), jax.ShapeDtypeStruct((2, 4, 128, 128), BF16)],
        in_specs=[VMEM, ANY, ANY, ANY],
        out_specs=[VMEM, VMEM],
        scratch_shapes=[
            pltpu.VMEM((4, 512, 1024), BF16),
            pltpu.VMEM((4, 128, 1024), BF16),
            pltpu.VMEM((4, 4, 128, 1024), BF16),
            pltpu.VMEM((4, 1024, 768), BF16),
            pltpu.VMEM((512, 768), F32),
            DMA((7,)), DMA((3, 4)), DMA((3, 4)), DMA((6,)), DMA((6,)), DMA((6,)), DMA((6,)),
        ],
        compiler_params=params(0),
        name="project",
    )(ids, wide, wq, wkv)


def attend(ids, q, kv):
    return pl.pallas_call(
        attend_kernel,
        out_shape=jax.ShapeDtypeStruct((4, 144, 512), BF16),
        in_specs=[VMEM] * 3,
        out_specs=VMEM,
        scratch_shapes=[
            pltpu.VMEM((16, 2, 4, 128, 128), BF16),
            pltpu.VMEM((512, 256), BF16),
            pltpu.VMEM((4, 1, 512), F32),
            pltpu.VMEM((4, 1, 512), F32),
            pltpu.VMEM((4, 128, 512), F32),
            pltpu.VMEM((4, 128, 512), BF16),
            pltpu.VMEM((4, 128, 512), BF16),
            pltpu.VMEM((4, 16, 512), BF16),
            pltpu.VMEM((4, 16, 512), BF16),
            DMA((8,)), DMA((8,)), DMA((16,)), DMA((4,)), DMA((4,)), DMA, DMA,
        ],
        compiler_params=params(1),
        name="attend",
    )(ids, q, kv)


def gradient(ids, states, ctx, gain, grad, wout):
    return pl.pallas_call(
        grad_kernel,
        out_shape=[jax.ShapeDtypeStruct((16, 1024), F32), jax.ShapeDtypeStruct((8, 128), F32)],
        in_specs=[VMEM] * 6,
        out_specs=[VMEM, VMEM],
        scratch_shapes=[
            pltpu.VMEM((1024, 512), F32),
            pltpu.VMEM((2, 4, 128, 512), BF16),
            pltpu.VMEM((4, 128, 1024), BF16),
            pltpu.VMEM((4, 128, 1024), BF16),
            pltpu.VMEM((2, 128, 512), BF16),
            pltpu.VMEM((2, 128, 1024), BF16),
            pltpu.VMEM((2, 128, 512), BF16),
            pltpu.VMEM((2, 128, 1024), BF16),
            pltpu.VMEM((8, 16, 1024), BF16),
            pltpu.VMEM((8, 16, 1024), BF16),
            pltpu.VMEM((4, 16, 1024), F32),
            pltpu.VMEM((16, 1024), BF16),
            pltpu.VMEM((16, 16, 128), F32),
            pltpu.VMEM((4, 16, 128), F32),
            DMA((4,)), DMA((4,)), DMA((4,)), DMA((4,)), DMA((8,)), DMA((8,)), DMA((4,)), DMA((4,)),
            DMA((3,)), DMA, DMA((16,)), DMA((16,)), DMA((4,)), DMA((4,)),
        ],
        compiler_params=params(2),
        name="gradient",
    )(ids, states, ctx, gain, grad, wout)


def on_device(byte_states, byte_wide, patch_of, w_query, w_keyval, w_out, norm_gain, out_grad):
    q, kv = project(patch_of, byte_wide[0], w_query, w_keyval)
    ctx = attend(patch_of, q, kv)
    rows, gains = gradient(patch_of, byte_states[0], ctx, norm_gain.reshape(8, 128), out_grad[0], w_out)
    return rows, gains.reshape(1024)


def solution(mesh):
    return jax.shard_map(
        on_device,
        mesh=mesh,
        in_specs=(
            P("fsdp", "seq", None),
            P("fsdp", "seq", None),
            P("fsdp", "seq"),
            P("fsdp", None),
            P("fsdp", None),
            P("fsdp", None),
            P(),
            P("fsdp", "seq", None),
        ),
        out_specs=(P("seq", None), P()),
        check_vma=False,
    )
```

time: 850 us -> 152 us (0.18)
  waiting for transfers between devices: 367 us -> 0 us
  blocking collectives: 262 us -> 0 us
  Pallas kernels: 0 us -> 148 us
  matrix products: 117 us -> 0 us
  other arithmetic: 43 us -> 0 us
  local copies, waits for them, and re-layouts: 36.9 us -> 2.75 us
  between operations: 18.4 us -> 0.66 us
    reduce_scatter x2 -> x0, waiting for transfers between devices: 206 us -> none  [the longest x1 137 us: on_device(): lax.psum_scatter(lax.dot_general(decoded, cotangent, (((0,), (0,)), ((),...]
    psum x2 -> x0, blocking collectives: 201 us -> none  [the longest x1 125 us: on_device(): square_sum = lax.psum(jnp.sum(weight_rows * weight_rows), 'seq')]
    all_gather x3 -> x0, waiting for transfers between devices: 155 us -> none  [the longest x1 83.1 us: on_device(): lax.all_gather(value_rows, 'seq', axis=0, tiled=True)]
    pallas_call x0 -> x3, Pallas kernels: none -> 148 us  [the longest x1 51.2 us: gradient(): pl.pallas_call(grad_kernel, out_shape=[jax.ShapeDtypeStruct((16, 1024), F...]
    dot_general x39 -> x0, matrix products: 117 us -> none  [the longest x16 57.4 us: attend_block(): jnp.einsum('kgqr,rke->kgqe', expo.astype(jnp.bfloat16).reshape(HK, group_...]
    all_gather x1 -> x0, blocking collectives: 41.8 us -> none  [on_device(): lax.all_gather(live_mask, 'seq', axis=0, tiled=True)]
    dynamic_slice x49 -> x0, local copies, waits for them, and re-layouts: 27.4 us -> none  [the longest x32 23.8 us: step_block(): lax.dynamic_slice_in_dim(value_piece, block_start, block, 0)]
    reduce_sum x22 -> x0, other arithmetic: 20.3 us -> none  [the longest x16 14.1 us: attend_block(): new_total = run_total * decay + jnp.sum(expo, axis=2)]
  transfers between devices with their start and end apart: 7 -> 0, of which waited for: 6 -> 0; matrix products, arithmetic and copies ran while one was open for 1% -> 0% of each run, Pallas kernels for 0% -> 0%
where the time goes in v1:
time: 152 us
  Pallas kernels  148 us (97%)
  local copies, waits for them, and re-layouts  2.75 us (2%)
    pallas_call x1, Pallas kernels, gradient(): pl.pallas_call(grad_kernel, out_shape=[jax.ShapeDtypeStruct((16, 1024), F...  51.2 us
    pallas_call x1, Pallas kernels, attend(): pl.pallas_call(attend_kernel, out_shape=jax.ShapeDtypeStruct((4, 144, 512...  51.1 us
    pallas_call x1, Pallas kernels, project(): pl.pallas_call(project_kernel, out_shape=[jax.ShapeDtypeStruct((4, 512, 2...  46.1 us

profile of v1, /device:TPU:1, one launch (start us, length us, event | category | flops | bytes accessed | tf_op | source)
XLA Modules:
  0.0 151.8 jit_solution(11903838601891729982)
XLA Ops:
  0.6 46.1 %project.1 = (bf16[4,512,256]{2,1,0:T(8,128)(2,1)}, bf16[2,4,128,128]{3,2,1,0:T(8,128)(2,1)}) custom-call(s32[1,512]{1,0:T(1,128)} %ids_ref.5, bf16[512,4096]{1,0:T(8,128)(2,1)} %bitcast.5, bf16[1024,2048]{1,0:T(8,128)(2,1)} %wq_ref.1, bf16[1024,1024]{1,0:T(8,128)(2,1)} %wkv_ref.1), custom_call_target="tpu_custom_call" | custom-call | tf_op jit(solution)/shard_map/project/pallas_call | solution.py:499
  46.7 51.1 %attend.1.ctx_ref = bf16[4,144,512]{2,1,0:T(8,128)(2,1)} custom-call(s32[1,512]{1,0:T(1,128)} %ids_ref.5, bf16[4,512,256]{2,1,0:T(8,128)(2,1)} %get-tuple-element.6.q_ref, bf16[2,4,128,128]{3,2,1,0:T(8,128)(2,1)} %get-tuple-element.7.kv_ref), custom_call_target="tpu_custom_call" | custom-call | tf_op jit(solution)/shard_map/attend/pallas_call | solution.py:518
  97.8 51.2 %gradient.1 = (f32[16,1024]{1,0:T(8,128)}, f32[8,128]{1,0:T(8,128)}) custom-call(s32[1,512]{1,0:T(1,128)} %ids_ref.5, bf16[512,1024]{1,0:T(8,128)(2,1)} %bitcast.6, bf16[4,144,512]{2,1,0:T(8,128)(2,1)} %attend.1.ctx_ref, f32[8,128]{1,0:T(8,128)} %bitcast.8, bf16[512,1024]{1,0:T(8,128)(2,1)} %bitcast.7, bf16[256,1024]{1,0:T(8,128)(2,1)} %wout_ref.1), custom_call_target="tpu_custom_call" | custom-call | tf_op jit(solution)/shard_map/gradient/pallas_call | solution.py:541
  149.1 1.5 copy.12
  150.5 1.3 copy.13

commit v2 on v1

v2 whole, which is shorter than its diff:
```python
import jax
import jax.numpy as jnp
from jax import lax
from jax.experimental import pallas as pl
from jax.experimental.pallas import tpu as pltpu
from jax.sharding import PartitionSpec as P

E = 128
PCAP = 128
NY, NZ, NX = 4, 8, 4
EPS = 1e-05
DEAD_ROW = 1024.0
DEAD_KEY = 4096.0
NEG = -1e30
Q_SCALE = float(E) ** (-0.5) * 1.4426950408889634
MESH = pl.DeviceIdType.MESH
F32 = jnp.float32
BF16 = jnp.bfloat16


def place():
    seq = lax.axis_index("seq")
    return seq // 16, (seq // 2) % 8, seq % 2, lax.axis_index("fsdp")


def dev(y, z, c, x):
    return {"seq": (y * 8 + z) * 2 + c, "fsdp": x}


def remote(src, dst, send, recv, peer):
    return pltpu.make_async_remote_copy(
        src_ref=src, dst_ref=dst, send_sem=send, recv_sem=recv, device_id=peer, device_id_type=MESH
    )


def dot(a, b, ca=1, cb=0):
    return lax.dot_general(a, b, (((ca,), (cb,)), ((), ())), preferred_element_type=F32)


def iota(shape, axis):
    return lax.broadcasted_iota(jnp.int32, shape, axis)


STEPS = (0, 3, 1, 2)


def window_kernel(ids_ref, gain_ref, wide_ref, wq_ref, wkv_ref, states_hbm, grad_hbm, wout_ref, out_ref, gout_ref,
                  wide_v, pooled, nrm, wbuf, accp, q_ref, blocks, kext, top, total, acc, osend, att, ctx_ref, row_out, row_in,
                  states_ref, grad_ref, sums_t, dec, sib_out, sib_in, xy_out, xy_in, z_out, z_in, xs, wrow, t0, t1, t2,
                  lsem, ysend, yrecv, xsend, xrecv, ssend, srecv, zrsend, zrsib, zrrecv, asend, arecv, rsend, rrecv,
                  sbsend, sbrecv, xysend, xyrecv, zsend, zrecv, gsend, grecv, wsend, wrecv, fsend, frecv):
    y, z, c, x = place()
    seq = lax.axis_index("seq")
    me = 2 * z + c
    right, left = dev((y + 1) % 4, z, c, x), dev((y + 3) % 4, z, c, x)
    xright, xleft = dev(y, z, c, (x + 1) % 4), dev(y, z, c, (x + 3) % 4)
    sibling = dev(y, z, 1 - c, x)
    ymates = [dev((y + d) % 4, z, c, x) for d in (1, 2, 3)]
    xmates = [dev(y, z, c, (x + d) % 4) for d in (1, 2, 3)]
    zmates = [dev(y, (z + d) % 8, c, x) for d in range(1, 8)]
    diagonals = [dev((y + dy) % 4, z, c, (x + dx) % 4) for dy in (1, 2, 3) for dx in (1, 2, 3)]
    following = {"seq": (seq + 1) % 64, "fsdp": x}
    before_me = {"seq": (seq + 63) % 64, "fsdp": x}
    dirn = 1 - 2 * c
    za, zb = dev(y, (z + dirn + 8) % 8, c, x), dev(y, (z - dirn + 8) % 8, c, x)
    peers = ymates + xmates + zmates + diagonals + [sibling, following, before_me]

    loads = [
        pltpu.make_async_copy(wide_ref.at[:, pl.ds(1024 * k, 1024)], wide_v.at[k], lsem.at[3 + k]) for k in range(4)
    ] + [
        pltpu.make_async_copy(wq_ref.at[:, pl.ds(pl.multiple_of(512 * y, 128), 512)], wbuf.at[0, :, pl.ds(0, 512)], lsem.at[0]),
        pltpu.make_async_copy(wkv_ref.at[:, pl.ds(pl.multiple_of(128 * y, 128), 128)], wbuf.at[0, :, pl.ds(512, 128)], lsem.at[1]),
        pltpu.make_async_copy(wkv_ref.at[:, pl.ds(pl.multiple_of(512 + 128 * y, 128), 128)], wbuf.at[0, :, pl.ds(640, 128)], lsem.at[2]),
        pltpu.make_async_copy(states_hbm, states_ref, lsem.at[7]),
        pltpu.make_async_copy(grad_hbm, grad_ref, lsem.at[8]),
    ]
    for load in loads:
        load.start()
    barrier = pltpu.get_barrier_semaphore()
    for peer in peers:
        pl.semaphore_signal(barrier, inc=1, device_id=peer, device_id_type=MESH)

    onehot = (iota((PCAP, 512), 0) == ids_ref[...]).astype(F32)
    sizes = jnp.sum(onehot, axis=1, keepdims=True)
    onehot = onehot.astype(BF16)
    inverse = 1.0 / jnp.maximum(sizes, 1.0)
    squares = jnp.zeros((PCAP, 1), F32)
    for k in range(4):
        loads[k].wait()
        chunk = (dot(onehot, wide_v[k]) * inverse).astype(BF16)
        pooled[k] = chunk
        chunk = chunk.astype(F32)
        squares = squares + jnp.sum(chunk * chunk, axis=1, keepdims=True)
    for load in loads[4:7]:
        load.wait()
    pl.semaphore_wait(barrier, len(peers))

    def part(slot, owner, half):
        return wbuf.at[slot, pl.ds(pl.multiple_of(512 * owner + 256 * half, 256), 256)]

    wsends = []
    for direction, peer in ((0, xright), (1, xleft)):
        for half in ((0, 1) if direction == 0 else (1, 0)):
            copy = remote(part(0, c, half), part(1 + direction, c, half),
                          xsend.at[2 * direction + half], xrecv.at[2 * direction + half], peer)
            copy.start()
            wsends.append(copy)

    scale = lax.rsqrt(squares / 4096.0 + EPS)
    rows = []
    for pair in ((0, 3), (1, 2)):
        for k in pair:
            chunk = pooled[k].astype(F32) * scale
            if k == 0:
                chunk = jnp.where((iota((PCAP, 1024), 1) == 0) & (sizes < 0.5), DEAD_ROW, chunk)
            nrm[k, 0] = chunk.astype(BF16)
            direction = 0 if k < 2 else 1
            copy = remote(nrm.at[k, 0], nrm.at[k, 1 + direction],
                          ysend.at[direction, k], yrecv.at[direction, k], (right, left)[direction])
            copy.start()
            rows.append((direction, k, copy))
    for direction, k in ((0, 2), (1, 1), (0, 3), (1, 0)):
        copy = remote(nrm.at[k, 0], nrm.at[k, 1 + direction],
                      ysend.at[direction, k], yrecv.at[direction, k], (right, left)[direction])
        copy.start()
        rows.append((direction, k, copy))
    wcopies = [remote(wout_ref.at[pl.ds(pl.multiple_of(16 * me, 16), 16)], wrow, wsend.at[d], wrecv, xmates[d]) for d in range(3)]
    wown = pltpu.make_async_copy(wout_ref.at[pl.ds(pl.multiple_of(16 * me, 16), 16)], wrow, lsem.at[9])

    @pl.when(x == y)
    def _():
        for copy in wcopies:
            copy.start()
        wown.start()

    arrivals = {(direction, k): copy for direction, k, copy in rows}
    warrivals = {(0, 0): wsends[0], (0, 1): wsends[1], (1, 1): wsends[2], (1, 0): wsends[3]}
    ysends = [copy for _, _, copy in rows]
    lasts, wlasts, ssends = [], [], []

    def give(slot, half):
        i = 2 * (slot - 1) + half
        copy = remote(part(slot, c, half), part(slot, c, half), ssend.at[i], srecv.at[i], sibling)
        copy.start()
        ssends.append(copy)

    def pass_rows(direction, k, peer):
        arrivals[direction, k].wait_recv()
        copy = remote(nrm.at[k, 1 + direction], nrm.at[k, 3], ysend.at[2, k], yrecv.at[2, k], peer)
        copy.start()
        lasts.append(copy)

    def pass_weights(direction, half, peer):
        warrivals[direction, half].wait_recv()
        if peer is not None:
            copy = remote(part(1 + direction, c, half), part(3, c, half), xsend.at[4 + half], xrecv.at[4 + half], peer)
            copy.start()
            wlasts.append(copy)
        give(1 + direction, half)

    pass_weights(0, 0, xright)
    pass_weights(1, 1, xleft)
    pass_rows(0, 0, right)
    pass_rows(1, 3, left)
    pass_rows(0, 1, right)
    pass_rows(1, 2, left)
    pass_weights(0, 1, None)
    pass_weights(1, 0, None)
    for half, copy in enumerate(wlasts):
        copy.wait_recv()
        give(3, half)
    for direction, k in ((0, 2), (1, 1), (0, 3), (1, 0)):
        arrivals[direction, k].wait_recv()
    for slot in (1, 2, 3):
        for half in range(2):
            i = 2 * (slot - 1) + half
            remote(part(slot, 1 - c, half), part(slot, 1 - c, half), ssend.at[i], srecv.at[i], sibling).wait_recv()

    ones = (iota((512, 128), 1) == 0).astype(F32).astype(BF16)
    first = []

    def publish(p):
        at = (y + STEPS[p]) % 4
        here = pl.ds(128 * p, 128)
        dead = nrm[0, p][:, 0:128].astype(F32)[:, 0:1] > 512.0
        blocks[0, at, 0] = jnp.where(dead, DEAD_KEY, accp[here, pl.ds(512, 128)]).astype(BF16)
        blocks[0, at, 1] = accp[here, pl.ds(640, 128)].T.astype(BF16)
        for copy in (
            remote(blocks.at[0, at], blocks.at[1, at], zrsend.at[1, p], zrrecv.at[1, p], za),
            remote(blocks.at[0, at], blocks.at[2, at], zrsend.at[2, p], zrrecv.at[2, p], zb),
            remote(blocks.at[0, at], blocks.at[8, at], zrsib.at[0, p], zrrecv.at[8, p], sibling),
        ):
            copy.start()
            first.append(copy)

    def queries(p):
        at = (y + STEPS[p]) % 4
        here = pl.ds(128 * p, 128)
        for g in range(4):
            q_ref[at, pl.ds(128 * g, 128), pl.ds(0, 128)] = (accp[here, pl.ds(128 * g, 128)] * Q_SCALE).astype(BF16)
        q_ref[at, :, pl.ds(128, 128)] = ones

    for at, step in enumerate(STEPS):
        k = (x + step) % 4
        value = dot(nrm[k, 0:3].reshape(384, 1024), wbuf[at])
        if at == 0:
            accp[0:384] = value
        else:
            accp[0:384] += value
    for p in range(3):
        publish(p)
    for p in range(3):
        queries(p)
    for copy in lasts:
        copy.wait_recv()
    for at, step in enumerate(STEPS):
        k = (x + step) % 4
        value = dot(nrm[k, 3], wbuf[at])
        if at == 0:
            accp[384:512] = value
        else:
            accp[384:512] += value
    publish(3)
    queries(3)

    def load_keys(slot):
        for i in range(4):
            keys = blocks[slot, i, 0]
            here = pl.ds(128 * i, 128)
            kext[here, 0:128] = keys
            dead = keys.astype(F32)[:, 0:1] > 2000.0
            kext[here, 128:256] = jnp.broadcast_to(jnp.where(dead, NEG, 0.0), (128, 128)).astype(BF16)

    def group(slot, work, fresh):
        def score(item):
            yq, count = item
            return dot(kext[0:128 * count], q_ref[yq], 1, 1)

        def soften(item, scores):
            yq, count = item
            if fresh:
                last = scores[128 * (count - 1):]
                allowed = iota((128, 512), 0) <= iota((128, 512), 1) % 128
                last = jnp.where(allowed, last, NEG)
                scores = jnp.concatenate([scores[: 128 * (count - 1)], last], axis=0) if count > 1 else last
            peak = jnp.max(scores, axis=0, keepdims=True)
            decay = None
            if not fresh:
                old = top[yq]
                peak = jnp.maximum(peak, old)
                decay = jnp.exp2(old - peak)
            probs = jnp.exp2(scores - peak)
            sums = jnp.sum(probs, axis=0, keepdims=True)
            top[yq] = peak
            total[yq] = sums if fresh else total[yq] * decay + sums
            return probs.astype(BF16), decay

        def mix(item, probs, decay):
            yq, count = item
            values = jnp.concatenate([blocks[slot, i, 1] for i in range(count)], axis=1)
            mixed = dot(values, probs)
            acc[yq] = mixed if fresh else acc[yq] * decay + mixed

        ahead, held = score(work[0]), None
        for i, item in enumerate(work):
            scores = ahead
            if i + 1 < len(work):
                ahead = score(work[i + 1])
            softened = soften(item, scores)
            if held is not None:
                mix(*held)
            held = (item, *softened)
        mix(*held)

    load_keys(0)
    group(0, [(yq, yq + 1) for yq in range(4)], True)

    def ring(i, carry):
        s = (i + 1) // 2
        sib = (i + 1) % 2
        slot = s + 8 * sib
        hop = (s + 1) // 2
        odd = s % 2
        step = dirn * (2 * odd - 1)
        onward = dev(y, (z + step + 8) % 8, c, x)
        for p in range(4):
            at = (y + STEPS[p]) % 4
            remote(blocks.at[slot, at], blocks.at[slot, at], zrsend.at[1, p], zrrecv.at[slot, p], sibling).wait_recv()

            @pl.when((sib == 0) & (s <= 5))
            def _():
                remote(blocks.at[s, at], blocks.at[s + 2, at], zrsend.at[s + 2, p], zrrecv.at[s + 2, p], onward).start()

            @pl.when(sib == 0)
            def _():
                remote(blocks.at[s, at], blocks.at[8 + s, at], zrsib.at[s, p], zrrecv.at[8 + s, p], sibling).start()

        back = hop * dirn * (1 - 2 * sib) * (2 * odd - 1)
        zsrc = (z - back + 8) % 8
        csrc = (1 - sib) * c + sib * (1 - c)
        earlier = 2 * zsrc + csrc < 2 * z + c
        load_keys(slot)

        @pl.when(earlier)
        def _():
            group(slot, [(yq, yq + 1) for yq in range(4)], False)

        @pl.when(jnp.logical_not(earlier))
        def _():
            group(slot, [(yq, yq) for yq in range(1, 4)], False)

        return carry

    lax.fori_loop(0, 15, ring, 0)

    for yq in range(4):
        out = acc[yq] / total[yq]
        for g in range(4):
            osend[yq, :, pl.ds(128 * g, 128)] = out[:, 128 * g:128 * g + 128].T.astype(BF16)
    backs = []
    for d in (2, 1, 3):
        copy = remote(osend.at[(y + d) % 4], att.at[y], asend.at[d], arecv.at[d], ymates[d - 1])
        copy.start()
        backs.append(copy)
    att[y] = osend[y]
    for d in (1, 3, 2):
        there = (y + 4 - d) % 4
        remote(att.at[there], att.at[there], asend.at[d], arecv.at[d], ymates[d - 1]).wait_recv()

    squares = jnp.zeros((PCAP, 1), F32)
    for h in range(4):
        piece = att[h].astype(F32)
        squares = squares + jnp.sum(piece * piece, axis=1, keepdims=True)
    scale = lax.rsqrt(squares / 2048.0 + EPS)
    ids = ids_ref[...]
    final = jnp.max(ids.astype(F32), axis=1, keepdims=True).astype(jnp.int32)
    pick = (iota((16, PCAP), 1) == final).astype(F32).astype(BF16)
    for h in range(4):
        ctx = (att[h].astype(F32) * scale).astype(BF16)
        ctx_ref[h, 0:128] = ctx
        row_out[h] = dot(pick, ctx).astype(BF16)
    row_copy = remote(row_out, row_in, rsend, rrecv, following)
    row_copy.start()
    for load in loads[7:]:
        load.wait()

    own_hot = iota((144, 512), 0) == ids
    prior_hot = iota((144, 512), 0) == jnp.where(ids > 0, ids - 1, 128)
    has_prior = (ids > 0) | (seq > 0)
    row_copy.wait_recv()
    for h in range(4):
        ctx_ref[h, 128:144] = row_in[h]
    squares = jnp.zeros((1, 512), F32)
    for h in range(8):
        lanes = pl.ds(128 * (h % 4), 128)
        states = states_ref[:, pl.ds(128 * h, 128)].astype(F32).T
        keys = ctx_ref[h // 4, :, lanes]
        values = ctx_ref[2 + h // 4, :, lanes]
        scores = dot(keys, states.astype(BF16)) * Q_SCALE
        own = jnp.sum(jnp.where(own_hot, scores, 0.0), axis=0, keepdims=True)
        prior = jnp.sum(jnp.where(prior_hot, scores, 0.0), axis=0, keepdims=True)
        prior = jnp.where(has_prior, prior, NEG)
        peak = jnp.maximum(own, prior)
        own = jnp.exp2(own - peak)
        prior = jnp.exp2(prior - peak)
        scale = 1.0 / (own + prior)
        weights = jnp.where(own_hot, own * scale, jnp.where(prior_hot, prior * scale, 0.0))
        attn = dot(values, weights.astype(BF16), 0, 0)
        summed = states + attn
        squares = squares + jnp.sum(summed * summed, axis=0, keepdims=True)
        sums_t[pl.ds(128 * h, 128)] = summed
    scale = lax.rsqrt(squares / 1024.0 + EPS)
    for h in range(8):
        gain = jnp.broadcast_to(gain_ref[h:h + 1], (128, 128)).T[:, 0:1]
        decoded = ((sums_t[pl.ds(128 * h, 128)] * scale) * gain).astype(BF16)
        for i in range(8):
            at = (h % 2) * 4 + i // 2
            dec[i % 2, h // 2, pl.ds(16 * at, 16)] = decoded[16 * i:16 * i + 16]

    sib_copies = []
    for i, d in enumerate((2, 1, 3, 0)):
        sib_out[i] = dot(dec[1 - c, (y + d) % 4], grad_ref[...]).astype(BF16)
        copy = remote(sib_out.at[i], sib_in.at[i], sbsend.at[i], sbrecv.at[i], sibling)
        copy.start()
        sib_copies.append(copy)
    xy_copies = []
    for i, d in enumerate((2, 1, 3, 0)):
        mine = dot(dec[c, (y + d) % 4], grad_ref[...])
        sib_copies[i].wait_recv()
        mine = mine + sib_in[i].astype(F32)
        for j in range(4):
            xy_out[d, j] = mine[:, 256 * j:256 * j + 256].astype(BF16)
        for e in (2, 1, 3, 0):
            if d == 0 and e == 0:
                continue
            peer = dev((y + d) % 4, z, c, (x + e) % 4)
            copy = remote(xy_out.at[d, (x + e) % 4], xy_in.at[4 * d + e], xysend.at[4 * d + e], xyrecv.at[4 * d + e], peer)
            copy.start()
            xy_copies.append((4 * d + e, copy))
    mine = xy_out[0, x].astype(F32)
    for i, copy in sorted(xy_copies, key=lambda pair: pair[0]):
        copy.wait_recv()
        mine = mine + xy_in[i].astype(F32)
    z_out[...] = mine.astype(BF16).reshape(8, 16, 256)
    z_copies = []
    for d in (4, 3, 5, 2, 6, 1, 7):
        copy = remote(z_out.at[(z + d) % 8], z_in.at[d], zsend.at[d], zrecv.at[d], zmates[d - 1])
        copy.start()
        z_copies.append((d, copy))
    piece = z_out[z].astype(F32)
    for d, copy in sorted(z_copies, key=lambda pair: pair[0]):
        copy.wait_recv()
        piece = piece + z_in[d].astype(F32)
    xs[x] = piece
    x_copies = []
    for d in (2, 1, 3):
        copy = remote(xs.at[x], xs.at[x], gsend.at[d], grecv.at[d], xmates[d - 1])
        copy.start()
        x_copies.append(copy)

    @pl.when(x == y)
    def _():
        wown.wait()

    @pl.when(x != y)
    def _():
        wcopies[0].wait_recv()

    for d in (1, 3, 2):
        there = (x + 4 - d) % 4
        remote(xs.at[there], xs.at[there], gsend.at[d], grecv.at[d], xmates[d - 1]).wait_recv()

    gains = jnp.zeros((16, 1), F32)
    parts = jnp.zeros((1, 128), F32)
    for j in range(4):
        piece = xs[j]
        gains = gains + jnp.sum(piece * wrow[:, pl.ds(256 * j, 256)].astype(F32), axis=1, keepdims=True)
        power = jnp.sum(piece * piece, axis=0, keepdims=True)
        parts = parts + (power[:, 0:128] + power[:, 128:256])
    lane = (z % 4) * 32 + c * 16
    spread = jnp.where(iota((16, 128), 1) == iota((16, 128), 0) + lane, gains, 0.0)
    spread = jnp.sum(spread, axis=0, keepdims=True)
    row = iota((8, 128), 0)
    t0[0, 0:8] = jnp.where(row == 2 * y + z // 4, spread, 0.0) / gain_ref[...]
    t0[0, 8:16] = jnp.where(row == 0, parts, 0.0)
    f_copies = [remote(t0.at[0], t0.at[1], fsend.at[0], frecv.at[0], sibling)]
    f_copies[0].start()
    f_copies[0].wait_recv()
    t1[z] = t0[0] + t0[1]
    for d in (4, 3, 5, 2, 6, 1, 7):
        copy = remote(t1.at[z], t1.at[z], fsend.at[d], frecv.at[d], zmates[d - 1])
        copy.start()
        f_copies.append(copy)
    for d in range(1, 8):
        there = (z + 8 - d) % 8
        remote(t1.at[there], t1.at[there], fsend.at[d], frecv.at[d], zmates[d - 1]).wait_recv()
    tile = t1[0]
    for i in range(1, 8):
        tile = tile + t1[i]
    t2[y] = tile
    for d in (2, 1, 3):
        copy = remote(t2.at[y], t2.at[y], fsend.at[7 + d], frecv.at[7 + d], ymates[d - 1])
        copy.start()
        f_copies.append(copy)
    for d in (1, 2, 3):
        there = (y + 4 - d) % 4
        remote(t2.at[there], t2.at[there], fsend.at[7 + d], frecv.at[7 + d], ymates[d - 1]).wait_recv()
    tile = (t2[0] + t2[1]) + (t2[2] + t2[3])
    gsum = tile[0:8]
    grand = jnp.sum(tile[8:16] + gsum * gsum, axis=0, keepdims=True)
    grand = jnp.sum(grand, axis=1, keepdims=True)
    clip = jnp.minimum(1.0, 1024.0 / jnp.sqrt(grand))
    for j in range(4):
        out_ref[:, pl.ds(256 * j, 256)] = xs[j] * clip
    gout_ref[...] = gsum * clip

    for copy in (wsends + wlasts + ysends + lasts + ssends + first + backs + [row_copy] + sib_copies + x_copies + f_copies
                 + [copy for _, copy in xy_copies] + [copy for _, copy in z_copies]):
        copy.wait_send()

    def drain(s, carry):
        for p in range(4):
            @pl.when(s >= 3)
            def _():
                remote(blocks.at[s, p], blocks.at[s, p], zrsend.at[s, p], zrrecv.at[s, p], sibling).wait_send()
            remote(blocks.at[s, p], blocks.at[s, p], zrsib.at[s, p], zrrecv.at[s, p], sibling).wait_send()
        return carry

    lax.fori_loop(1, 8, drain, 0)

    @pl.when(x == y)
    def _():
        for copy in wcopies:
            copy.wait_send()


VMEM = pl.BlockSpec(memory_space=pltpu.VMEM)
ANY = pl.BlockSpec(memory_space=pl.ANY)
DMA = pltpu.SemaphoreType.DMA


def window(ids, gain, wide, wq, wkv, states, grad, wout):
    return pl.pallas_call(
        window_kernel,
        out_shape=[jax.ShapeDtypeStruct((16, 1024), F32), jax.ShapeDtypeStruct((8, 128), F32)],
        in_specs=[VMEM] * 2 + [ANY] * 6,
        out_specs=[VMEM, VMEM],
        scratch_shapes=[
            pltpu.VMEM((4, 512, 1024), BF16),
            pltpu.VMEM((4, 128, 1024), BF16),
            pltpu.VMEM((4, 4, 128, 1024), BF16),
            pltpu.VMEM((4, 1024, 768), BF16),
            pltpu.VMEM((512, 768), F32),
            pltpu.VMEM((4, 512, 256), BF16),
            pltpu.VMEM((16, 4, 2, 128, 128), BF16),
            pltpu.VMEM((512, 256), BF16),
            pltpu.VMEM((4, 1, 512), F32),
            pltpu.VMEM((4, 1, 512), F32),
            pltpu.VMEM((4, 128, 512), F32),
            pltpu.VMEM((4, 128, 512), BF16),
            pltpu.VMEM((4, 128, 512), BF16),
            pltpu.VMEM((4, 144, 512), BF16),
            pltpu.VMEM((4, 16, 512), BF16),
            pltpu.VMEM((4, 16, 512), BF16),
            pltpu.VMEM((512, 1024), BF16),
            pltpu.VMEM((512, 1024), BF16),
            pltpu.VMEM((1024, 512), F32),
            pltpu.VMEM((2, 4, 128, 512), BF16),
            pltpu.VMEM((4, 128, 1024), BF16),
            pltpu.VMEM((4, 128, 1024), BF16),
            pltpu.VMEM((4, 4, 128, 256), BF16),
            pltpu.VMEM((16, 128, 256), BF16),
            pltpu.VMEM((8, 16, 256), BF16),
            pltpu.VMEM((8, 16, 256), BF16),
            pltpu.VMEM((4, 16, 256), F32),
            pltpu.VMEM((16, 1024), BF16),
            pltpu.VMEM((2, 16, 128), F32),
            pltpu.VMEM((8, 16, 128), F32),
            pltpu.VMEM((4, 16, 128), F32),
            DMA((10,)), DMA((3, 4)), DMA((3, 4)), DMA((6,)), DMA((6,)), DMA((6,)), DMA((6,)),
            DMA((8, 4)), DMA((8, 4)), DMA((16, 4)), DMA((4,)), DMA((4,)), DMA, DMA,
            DMA((4,)), DMA((4,)), DMA((16,)), DMA((16,)), DMA((8,)), DMA((8,)), DMA((4,)), DMA((4,)),
            DMA((3,)), DMA, DMA((11,)), DMA((11,)),
        ],
        compiler_params=pltpu.CompilerParams(collective_id=0, has_side_effects=True, vmem_limit_bytes=56 * 1024 * 1024),
        name="window",
    )(ids, gain, wide, wq, wkv, states, grad, wout)


def finish_kernel(rows_ref, gains_ref, out_ref, gout_ref):
    out_ref[...] = rows_ref[...]
    gout_ref[...] = gains_ref[...]


def finish(rows, gains):
    return pl.pallas_call(
        finish_kernel,
        out_shape=[jax.ShapeDtypeStruct((16, 1024), F32), jax.ShapeDtypeStruct((8, 128), F32)],
        in_specs=[VMEM, VMEM],
        out_specs=[VMEM, VMEM],
        name="finish",
    )(rows, gains)


def on_device(byte_states, byte_wide, patch_of, w_query, w_keyval, w_out, norm_gain, out_grad):
    rows, gains = finish(*window(
        patch_of, norm_gain.reshape(8, 128), byte_wide[0], w_query, w_keyval, byte_states[0], out_grad[0], w_out
    ))
    return rows, gains.reshape(1024)


def solution(mesh):
    return jax.shard_map(
        on_device,
        mesh=mesh,
        in_specs=(
            P("fsdp", "seq", None),
            P("fsdp", "seq", None),
            P("fsdp", "seq"),
            P("fsdp", None),
            P("fsdp", None),
            P("fsdp", None),
            P(),
            P("fsdp", "seq", None),
        ),
        out_specs=(P("seq", None), P()),
        check_vma=False,
    )
```

time: 152 us -> 129 us (0.85)
  Pallas kernels: 148 us -> 129 us
  local copies, waits for them, and re-layouts: 2.75 us -> 0 us
    pallas_call x3 -> x2, Pallas kernels: 148 us -> 129 us  [the longest x1 127 us: window(): pl.pallas_call(window_kernel, out_shape=[jax.ShapeDtypeStruct((16, 1024),...]
    unnamed x2 -> x0, local copies, waits for them, and re-layouts: 2.75 us -> none
where the time goes in v2:
time: 129 us
  Pallas kernels  129 us (100%)
    pallas_call x1, Pallas kernels, window(): pl.pallas_call(window_kernel, out_shape=[jax.ShapeDtypeStruct((16, 1024),...  127 us

profile of v2, /device:TPU:1, one launch (start us, length us, event | category | flops | bytes accessed | tf_op | source)
XLA Modules:
  0.0 129.3 jit_solution(17457186420375404553)
XLA Ops:
  0.6 127.1 %window.1 = (f32[16,1024]{1,0:T(8,128)}, f32[8,128]{1,0:T(8,128)}) custom-call(s32[1,512]{1,0:T(1,128)} %ids_ref.1, f32[8,128]{1,0:T(8,128)} %bitcast.8, bf16[512,4096]{1,0:T(8,128)(2,1)} %bitcast.5, bf16[1024,2048]{1,0:T(8,128)(2,1)} %wq_ref.1, bf16[1024,1024]{1,0:T(8,128)(2,1)} %wkv_ref.1, bf16[512,1024]{1,0:T(8,128)(2,1)} %bitcast.6, ...), custom_call_target="tpu_custom_call" | custom-call | tf_op jit(solution)/shard_map/window/pallas_call | solution.py:503
  127.8 1.5 %finish.1 = (f32[16,1024]{1,0:T(8,128)}, f32[8,128]{1,0:T(8,128)}) custom-call(f32[16,1024]{1,0:T(8,128)} %get-tuple-element.6.rows_ref, f32[8,128]{1,0:T(8,128)} %get-tuple-element.7.gains_ref), custom_call_target="tpu_custom_call" | custom-call | tf_op jit(solution)/shard_map/finish/pallas_call | solution.py:556

commit v3 on v2

--- a/solution.py
+++ b/solution.py
@@ -45,9 +45,9 @@
 
 
 def window_kernel(ids_ref, gain_ref, wide_ref, wq_ref, wkv_ref, states_hbm, grad_hbm, wout_ref, out_ref, gout_ref,
-                  wide_v, pooled, nrm, wbuf, accp, q_ref, blocks, kext, top, total, acc, osend, att, ctx_ref, row_out, row_in,
+                  wide_v, pooled, nrm, wbuf, accp, q_ref, blocks, kext, top, total, acc, osend, att, ctx_ref, picks, row_out, row_in,
                   states_ref, grad_ref, sums_t, dec, sib_out, sib_in, xy_out, xy_in, z_out, z_in, xs, wrow, t0, t1, t2,
-                  lsem, ysend, yrecv, xsend, xrecv, ssend, srecv, zrsend, zrsib, zrrecv, asend, arecv, rsend, rrecv,
+                  lsem, ysend, yrecv, xsend, xrecv, ssend, srecv, wzsend, wzrecv, zrsend, zrsib, zrrecv, asend, arecv, rsend, rrecv,
                   sbsend, sbrecv, xysend, xyrecv, zsend, zrecv, gsend, grecv, wsend, wrecv, fsend, frecv):
     y, z, c, x = place()
     seq = lax.axis_index("seq")
@@ -59,11 +59,11 @@
     xmates = [dev(y, z, c, (x + d) % 4) for d in (1, 2, 3)]
     zmates = [dev(y, (z + d) % 8, c, x) for d in range(1, 8)]
     diagonals = [dev((y + dy) % 4, z, c, (x + dx) % 4) for dy in (1, 2, 3) for dx in (1, 2, 3)]
-    following = {"seq": (seq + 1) % 64, "fsdp": x}
-    before_me = {"seq": (seq + 63) % 64, "fsdp": x}
+    followers = [{"seq": (16 * i + me + 1) % 64, "fsdp": x} for i in range(4)]
+    leaders = [{"seq": (16 * i + me + 63) % 64, "fsdp": x} for i in range(4)]
     dirn = 1 - 2 * c
     za, zb = dev(y, (z + dirn + 8) % 8, c, x), dev(y, (z - dirn + 8) % 8, c, x)
-    peers = ymates + xmates + zmates + diagonals + [sibling, following, before_me]
+    peers = ymates + xmates + zmates + diagonals + followers + leaders + [sibling]
 
     loads = [
         pltpu.make_async_copy(wide_ref.at[:, pl.ds(1024 * k, 1024)], wide_v.at[k], lsem.at[3 + k]) for k in range(4)
@@ -95,35 +95,39 @@
         load.wait()
     pl.semaphore_wait(barrier, len(peers))
 
-    def part(slot, owner, half):
-        return wbuf.at[slot, pl.ds(pl.multiple_of(512 * owner + 256 * half, 256), 256)]
-
-    wsends = []
-    for direction, peer in ((0, xright), (1, xleft)):
-        for half in ((0, 1) if direction == 0 else (1, 0)):
-            copy = remote(part(0, c, half), part(1 + direction, c, half),
-                          xsend.at[2 * direction + half], xrecv.at[2 * direction + half], peer)
-            copy.start()
-            wsends.append(copy)
-
-    scale = lax.rsqrt(squares / 4096.0 + EPS)
-    rows = []
-    for pair in ((0, 3), (1, 2)):
-        for k in pair:
-            chunk = pooled[k].astype(F32) * scale
-            if k == 0:
-                chunk = jnp.where((iota((PCAP, 1024), 1) == 0) & (sizes < 0.5), DEAD_ROW, chunk)
-            nrm[k, 0] = chunk.astype(BF16)
-            direction = 0 if k < 2 else 1
-            copy = remote(nrm.at[k, 0], nrm.at[k, 1 + direction],
-                          ysend.at[direction, k], yrecv.at[direction, k], (right, left)[direction])
-            copy.start()
-            rows.append((direction, k, copy))
-    for direction, k in ((0, 2), (1, 1), (0, 3), (1, 0)):
+    parity = z % 2
+
+    def part(slot, owner, side, half):
+        return wbuf.at[slot, pl.ds(pl.multiple_of(512 * owner + 256 * side + 128 * half, 128), 128)]
+
+    def send_weights(direction, half):
+        i = 2 * direction + half
+        copy = remote(part(0, c, parity, half), part(1 + direction, c, parity, half),
+                      xsend.at[i], xrecv.at[i], (xright, xleft)[direction])
+        copy.start()
+        return copy
+
+    def send_rows(direction, k):
         copy = remote(nrm.at[k, 0], nrm.at[k, 1 + direction],
                       ysend.at[direction, k], yrecv.at[direction, k], (right, left)[direction])
         copy.start()
-        rows.append((direction, k, copy))
+        return copy
+
+    warrivals = {}
+    for half in range(2):
+        for direction in range(2):
+            warrivals[direction, half ^ direction] = send_weights(direction, half ^ direction)
+    scale = lax.rsqrt(squares / 4096.0 + EPS)
+    arrivals = {}
+    for k in (0, 3, 1, 2):
+        chunk = pooled[k].astype(F32) * scale
+        if k == 0:
+            chunk = jnp.where((iota((PCAP, 1024), 1) == 0) & (sizes < 0.5), DEAD_ROW, chunk)
+        nrm[k, 0] = chunk.astype(BF16)
+        direction = 0 if k < 2 else 1
+        arrivals[direction, k] = send_rows(direction, k)
+    for direction, k in ((0, 2), (1, 1), (0, 3), (1, 0)):
+        arrivals[direction, k] = send_rows(direction, k)
     wcopies = [remote(wout_ref.at[pl.ds(pl.multiple_of(16 * me, 16), 16)], wrow, wsend.at[d], wrecv, xmates[d]) for d in range(3)]
     wown = pltpu.make_async_copy(wout_ref.at[pl.ds(pl.multiple_of(16 * me, 16), 16)], wrow, lsem.at[9])
 
@@ -133,16 +137,20 @@
             copy.start()
         wown.start()
 
-    arrivals = {(direction, k): copy for direction, k, copy in rows}
-    warrivals = {(0, 0): wsends[0], (0, 1): wsends[1], (1, 1): wsends[2], (1, 0): wsends[3]}
-    ysends = [copy for _, _, copy in rows]
-    lasts, wlasts, ssends = [], [], []
-
-    def give(slot, half):
+    lasts, wlasts, zgives, ssends = [], [], [], []
+
+    def give(slot, side, half, i):
+        copy = remote(part(slot, c, side, half), part(slot, c, side, half), ssend.at[i], srecv.at[i], sibling)
+        copy.start()
+        ssends.append(copy)
+
+    def spread_weights(slot, half):
         i = 2 * (slot - 1) + half
-        copy = remote(part(slot, c, half), part(slot, c, half), ssend.at[i], srecv.at[i], sibling)
-        copy.start()
-        ssends.append(copy)
+        copy = remote(part(slot, c, parity, half), part(slot, c, parity, half), wzsend.at[i], wzrecv.at[i],
+                      zmates[0] if half == 0 else zmates[6])
+        copy.start()
+        zgives.append((slot, half, copy))
+        give(slot, parity, half, i)
 
     def pass_rows(direction, k, peer):
         arrivals[direction, k].wait_recv()
@@ -150,31 +158,30 @@
         copy.start()
         lasts.append(copy)
 
-    def pass_weights(direction, half, peer):
+    for direction, half in ((0, 0), (1, 1), (0, 1), (1, 0)):
         warrivals[direction, half].wait_recv()
-        if peer is not None:
-            copy = remote(part(1 + direction, c, half), part(3, c, half), xsend.at[4 + half], xrecv.at[4 + half], peer)
+        if direction == half:
+            copy = remote(part(1 + direction, c, parity, half), part(3, c, parity, half),
+                          xsend.at[4 + half], xrecv.at[4 + half], (xright, xleft)[direction])
             copy.start()
             wlasts.append(copy)
-        give(1 + direction, half)
-
-    pass_weights(0, 0, xright)
-    pass_weights(1, 1, xleft)
+        spread_weights(1 + direction, half)
+    for half, copy in enumerate(wlasts):
+        copy.wait_recv()
+        spread_weights(3, half)
+    for slot, half, copy in zgives:
+        copy.wait_recv()
+        give(slot, 1 - parity, half, 6 + 2 * (slot - 1) + half)
     pass_rows(0, 0, right)
     pass_rows(1, 3, left)
     pass_rows(0, 1, right)
     pass_rows(1, 2, left)
-    pass_weights(0, 1, None)
-    pass_weights(1, 0, None)
-    for half, copy in enumerate(wlasts):
-        copy.wait_recv()
-        give(3, half)
     for direction, k in ((0, 2), (1, 1), (0, 3), (1, 0)):
         arrivals[direction, k].wait_recv()
-    for slot in (1, 2, 3):
-        for half in range(2):
-            i = 2 * (slot - 1) + half
-            remote(part(slot, 1 - c, half), part(slot, 1 - c, half), ssend.at[i], srecv.at[i], sibling).wait_recv()
+    for copy in ssends:
+        copy.wait_recv()
+    wsends = list(warrivals.values()) + [copy for _, _, copy in zgives]
+    ysends = list(arrivals.values())
 
     ones = (iota((512, 128), 1) == 0).astype(F32).astype(BF16)
     first = []
@@ -183,6 +190,8 @@
         at = (y + STEPS[p]) % 4
         here = pl.ds(128 * p, 128)
         dead = nrm[0, p][:, 0:128].astype(F32)[:, 0:1] > 512.0
+        living = jnp.sum(jnp.where(dead, 0.0, 1.0), axis=0, keepdims=True).astype(jnp.int32)
+        picks[at] = (iota((16, PCAP), 1) == living - 1).astype(F32).astype(BF16)
         blocks[0, at, 0] = jnp.where(dead, DEAD_KEY, accp[here, pl.ds(512, 128)]).astype(BF16)
         blocks[0, at, 1] = accp[here, pl.ds(640, 128)].T.astype(BF16)
         for copy in (
@@ -199,6 +208,37 @@
         for g in range(4):
             q_ref[at, pl.ds(128 * g, 128), pl.ds(0, 128)] = (accp[here, pl.ds(128 * g, 128)] * Q_SCALE).astype(BF16)
         q_ref[at, :, pl.ds(128, 128)] = ones
+
+    def arrived(slot, p):
+        at = (y + STEPS[p]) % 4
+        remote(blocks.at[slot, at], blocks.at[slot, at], zrsend.at[1, p], zrrecv.at[slot, p], sibling).wait_recv()
+
+    def relay(slot, p, peer):
+        at = (y + STEPS[p]) % 4
+        remote(blocks.at[slot, at], blocks.at[slot + 2, at], zrsend.at[slot + 2, p], zrrecv.at[slot + 2, p], peer).start()
+
+    def share(slot, p):
+        at = (y + STEPS[p]) % 4
+        remote(blocks.at[slot, at], blocks.at[8 + slot, at], zrsib.at[slot, p], zrrecv.at[8 + slot, p], sibling).start()
+
+    def handle(hop, p):
+        arrived(2 * hop - 1, p)
+
+        @pl.when(hop <= 3)
+        def _():
+            relay(2 * hop - 1, p, za)
+
+        share(2 * hop - 1, p)
+
+        @pl.when(hop <= 3)
+        def _():
+            arrived(2 * hop, p)
+
+            @pl.when(hop <= 2)
+            def _():
+                relay(2 * hop, p, zb)
+
+            share(2 * hop, p)
 
     for at, step in enumerate(STEPS):
         k = (x + step) % 4
@@ -211,6 +251,8 @@
         publish(p)
     for p in range(3):
         queries(p)
+    for p in range(3):
+        handle(1, p)
     for copy in lasts:
         copy.wait_recv()
     for at, step in enumerate(STEPS):
@@ -223,26 +265,27 @@
     publish(3)
     queries(3)
 
-    def load_keys(slot):
+    def load_keys(slots):
         for i in range(4):
-            keys = blocks[slot, i, 0]
-            here = pl.ds(128 * i, 128)
-            kext[here, 0:128] = keys
-            dead = keys.astype(F32)[:, 0:1] > 2000.0
-            kext[here, 128:256] = jnp.broadcast_to(jnp.where(dead, NEG, 0.0), (128, 128)).astype(BF16)
-
-    def group(slot, work, fresh):
+            for j, slot in enumerate(slots):
+                keys = blocks[slot, i, 0]
+                here = pl.ds(256 * i + 128 * j, 128)
+                kext[here, 0:128] = keys
+                dead = keys.astype(F32)[:, 0:1] > 2000.0
+                kext[here, 128:256] = jnp.broadcast_to(jnp.where(dead, NEG, 0.0), (128, 128)).astype(BF16)
+
+    def group(slots, work, fresh):
         def score(item):
             yq, count = item
-            return dot(kext[0:128 * count], q_ref[yq], 1, 1)
+            return dot(kext[0:256 * count], q_ref[yq], 1, 1)
 
         def soften(item, scores):
             yq, count = item
             if fresh:
-                last = scores[128 * (count - 1):]
-                allowed = iota((128, 512), 0) <= iota((128, 512), 1) % 128
-                last = jnp.where(allowed, last, NEG)
-                scores = jnp.concatenate([scores[: 128 * (count - 1)], last], axis=0) if count > 1 else last
+                last = scores[256 * (count - 1):]
+                reach = jnp.where(iota((256, 512), 0) < 128, iota((256, 512), 1) % 128, 255 * c)
+                last = jnp.where(iota((256, 512), 0) <= reach, last, NEG)
+                scores = jnp.concatenate([scores[: 256 * (count - 1)], last], axis=0) if count > 1 else last
             peak = jnp.max(scores, axis=0, keepdims=True)
             decay = None
             if not fresh:
@@ -257,7 +300,7 @@
 
         def mix(item, probs, decay):
             yq, count = item
-            values = jnp.concatenate([blocks[slot, i, 1] for i in range(count)], axis=1)
+            values = jnp.concatenate([blocks[slot, i, 1] for i in range(count) for slot in slots], axis=1)
             mixed = dot(values, probs)
             acc[yq] = mixed if fresh else acc[yq] * decay + mixed
 
@@ -272,46 +315,39 @@
             held = (item, *softened)
         mix(*held)
 
-    load_keys(0)
-    group(0, [(yq, yq + 1) for yq in range(4)], True)
+    for p in range(4):
+        arrived(8, p)
+    load_keys((0, 8))
+    group((0, 8), [(yq, yq + 1) for yq in range(4)], True)
 
     def ring(i, carry):
-        s = (i + 1) // 2
-        sib = (i + 1) % 2
-        slot = s + 8 * sib
-        hop = (s + 1) // 2
-        odd = s % 2
-        step = dirn * (2 * odd - 1)
-        onward = dev(y, (z + step + 8) % 8, c, x)
+        s = i + 1
+        hop = i // 2 + 1
+        odd = 1 - i % 2
+
+        @pl.when(odd == 0)
+        def _():
+            for p in range(4):
+                handle(hop + 1, p)
+
+        mate = 7 + s + 2 * odd - s // 7
         for p in range(4):
-            at = (y + STEPS[p]) % 4
-            remote(blocks.at[slot, at], blocks.at[slot, at], zrsend.at[1, p], zrrecv.at[slot, p], sibling).wait_recv()
-
-            @pl.when((sib == 0) & (s <= 5))
-            def _():
-                remote(blocks.at[s, at], blocks.at[s + 2, at], zrsend.at[s + 2, p], zrrecv.at[s + 2, p], onward).start()
-
-            @pl.when(sib == 0)
-            def _():
-                remote(blocks.at[s, at], blocks.at[8 + s, at], zrsib.at[s, p], zrrecv.at[8 + s, p], sibling).start()
-
-        back = hop * dirn * (1 - 2 * sib) * (2 * odd - 1)
-        zsrc = (z - back + 8) % 8
-        csrc = (1 - sib) * c + sib * (1 - c)
-        earlier = 2 * zsrc + csrc < 2 * z + c
-        load_keys(slot)
-
-        @pl.when(earlier)
+            arrived(mate, p)
+        zsrc = (z - hop * dirn * (2 * odd - 1) + 8) % 8
+        load_keys((s, mate))
+
+        @pl.when(zsrc < z)
         def _():
-            group(slot, [(yq, yq + 1) for yq in range(4)], False)
-
-        @pl.when(jnp.logical_not(earlier))
+            group((s, mate), [(yq, yq + 1) for yq in range(4)], False)
+
+        @pl.when(zsrc > z)
         def _():
-            group(slot, [(yq, yq) for yq in range(1, 4)], False)
+            group((s, mate), [(yq, yq) for yq in range(1, 4)], False)
 
         return carry
 
-    lax.fori_loop(0, 15, ring, 0)
+    handle(1, 3)
+    lax.fori_loop(0, 7, ring, 0)
 
     for yq in range(4):
         out = acc[yq] / total[yq]
@@ -322,6 +358,11 @@
         copy = remote(osend.at[(y + d) % 4], att.at[y], asend.at[d], arecv.at[d], ymates[d - 1])
         copy.start()
         backs.append(copy)
+    for yq in range(4):
+        row_out[yq] = dot(picks[yq], osend[yq]).astype(BF16)
+        copy = remote(row_out.at[yq], row_in.at[y], rsend.at[yq], rrecv.at[y], followers[yq])
+        copy.start()
+        backs.append(copy)
     att[y] = osend[y]
     for d in (1, 3, 2):
         there = (y + 4 - d) % 4
@@ -333,23 +374,23 @@
         squares = squares + jnp.sum(piece * piece, axis=1, keepdims=True)
     scale = lax.rsqrt(squares / 2048.0 + EPS)
     ids = ids_ref[...]
-    final = jnp.max(ids.astype(F32), axis=1, keepdims=True).astype(jnp.int32)
-    pick = (iota((16, PCAP), 1) == final).astype(F32).astype(BF16)
     for h in range(4):
-        ctx = (att[h].astype(F32) * scale).astype(BF16)
-        ctx_ref[h, 0:128] = ctx
-        row_out[h] = dot(pick, ctx).astype(BF16)
-    row_copy = remote(row_out, row_in, rsend, rrecv, following)
-    row_copy.start()
+        ctx_ref[h, 0:128] = (att[h].astype(F32) * scale).astype(BF16)
+    for h in range(4):
+        remote(row_in.at[h], row_in.at[h], rsend.at[h], rrecv.at[h], sibling).wait_recv()
+    squares = jnp.zeros((16, 1), F32)
+    for h in range(4):
+        piece = row_in[h].astype(F32)
+        squares = squares + jnp.sum(piece * piece, axis=1, keepdims=True)
+    scale = lax.rsqrt(squares / 2048.0 + EPS)
+    for h in range(4):
+        ctx_ref[h, 128:144] = (row_in[h].astype(F32) * scale).astype(BF16)
     for load in loads[7:]:
         load.wait()
 
     own_hot = iota((144, 512), 0) == ids
     prior_hot = iota((144, 512), 0) == jnp.where(ids > 0, ids - 1, 128)
     has_prior = (ids > 0) | (seq > 0)
-    row_copy.wait_recv()
-    for h in range(4):
-        ctx_ref[h, 128:144] = row_in[h]
     squares = jnp.zeros((1, 512), F32)
     for h in range(8):
         lanes = pl.ds(128 * (h % 4), 128)
@@ -474,7 +515,7 @@
         out_ref[:, pl.ds(256 * j, 256)] = xs[j] * clip
     gout_ref[...] = gsum * clip
 
-    for copy in (wsends + wlasts + ysends + lasts + ssends + first + backs + [row_copy] + sib_copies + x_copies + f_copies
+    for copy in (wsends + wlasts + ysends + lasts + ssends + first + backs + sib_copies + x_copies + f_copies
                  + [copy for _, copy in xy_copies] + [copy for _, copy in z_copies]):
         copy.wait_send()
 
@@ -513,13 +554,14 @@
             pltpu.VMEM((512, 768), F32),
             pltpu.VMEM((4, 512, 256), BF16),
             pltpu.VMEM((16, 4, 2, 128, 128), BF16),
-            pltpu.VMEM((512, 256), BF16),
+            pltpu.VMEM((1024, 256), BF16),
             pltpu.VMEM((4, 1, 512), F32),
             pltpu.VMEM((4, 1, 512), F32),
             pltpu.VMEM((4, 128, 512), F32),
             pltpu.VMEM((4, 128, 512), BF16),
             pltpu.VMEM((4, 128, 512), BF16),
             pltpu.VMEM((4, 144, 512), BF16),
+            pltpu.VMEM((4, 16, 128), BF16),
             pltpu.VMEM((4, 16, 512), BF16),
             pltpu.VMEM((4, 16, 512), BF16),
             pltpu.VMEM((512, 1024), BF16),
@@ -537,8 +579,8 @@
             pltpu.VMEM((2, 16, 128), F32),
             pltpu.VMEM((8, 16, 128), F32),
             pltpu.VMEM((4, 16, 128), F32),
-            DMA((10,)), DMA((3, 4)), DMA((3, 4)), DMA((6,)), DMA((6,)), DMA((6,)), DMA((6,)),
-            DMA((8, 4)), DMA((8, 4)), DMA((16, 4)), DMA((4,)), DMA((4,)), DMA, DMA,
+            DMA((10,)), DMA((3, 4)), DMA((3, 4)), DMA((6,)), DMA((6,)), DMA((12,)), DMA((12,)), DMA((6,)), DMA((6,)),
+            DMA((8, 4)), DMA((8, 4)), DMA((16, 4)), DMA((4,)), DMA((4,)), DMA((4,)), DMA((4,)),
             DMA((4,)), DMA((4,)), DMA((16,)), DMA((16,)), DMA((8,)), DMA((8,)), DMA((4,)), DMA((4,)),
             DMA((3,)), DMA, DMA((11,)), DMA((11,)),
         ],

time: 129 us -> 124 us (0.961)
  Pallas kernels: 129 us -> 123 us
    pallas_call x1, Pallas kernels: 127 us -> 122 us  [window(): pl.pallas_call(window_kernel, out_shape=[jax.ShapeDtypeStruct((16, 1024),...]
where the time goes in v3:
time: 124 us
  Pallas kernels  123 us (99%)
    pallas_call x1, Pallas kernels, window(): pl.pallas_call(window_kernel, out_shape=[jax.ShapeDtypeStruct((16, 1024),...  122 us

profile of v3, /device:TPU:1, one launch (start us, length us, event | category | flops | bytes accessed | tf_op | source)
XLA Modules:
  0.0 123.6 jit_solution(7523280298968934665)
XLA Ops:
  0.6 121.5 %window.1 = (f32[16,1024]{1,0:T(8,128)}, f32[8,128]{1,0:T(8,128)}) custom-call(s32[1,512]{1,0:T(1,128)} %ids_ref.1, f32[8,128]{1,0:T(8,128)} %bitcast.8, bf16[512,4096]{1,0:T(8,128)(2,1)} %bitcast.5, bf16[1024,2048]{1,0:T(8,128)(2,1)} %wq_ref.1, bf16[1024,1024]{1,0:T(8,128)(2,1)} %wkv_ref.1, bf16[512,1024]{1,0:T(8,128)(2,1)} %bitcast.6, ...), custom_call_target="tpu_custom_call" | custom-call | tf_op jit(solution)/shard_map/window/pallas_call | solution.py:544
  122.1 1.5 %finish.1 = (f32[16,1024]{1,0:T(8,128)}, f32[8,128]{1,0:T(8,128)}) custom-call(f32[16,1024]{1,0:T(8,128)} %get-tuple-element.6.rows_ref, f32[8,128]{1,0:T(8,128)} %get-tuple-element.7.gains_ref), custom_call_target="tpu_custom_call" | custom-call | tf_op jit(solution)/shard_map/finish/pallas_call | solution.py:598

commit v4 on v3

--- a/solution.py
+++ b/solution.py
@@ -46,9 +46,9 @@
 
 def window_kernel(ids_ref, gain_ref, wide_ref, wq_ref, wkv_ref, states_hbm, grad_hbm, wout_ref, out_ref, gout_ref,
                   wide_v, pooled, nrm, wbuf, accp, q_ref, blocks, kext, top, total, acc, osend, att, ctx_ref, picks, row_out, row_in,
-                  states_ref, grad_ref, sums_t, dec, sib_out, sib_in, xy_out, xy_in, z_out, z_in, xs, wrow, t0, t1, t2,
+                  states_ref, grad_ref, sums_t, dec, sib_out, sib_in, a_out, b_out, a_in, b_in, a_two, b_two, a_last, b_last, z_out, z_in, xs, wrow, t0, t1, t2,
                   lsem, ysend, yrecv, xsend, xrecv, ssend, srecv, wzsend, wzrecv, zrsend, zrsib, zrrecv, asend, arecv, rsend, rrecv,
-                  sbsend, sbrecv, xysend, xyrecv, zsend, zrecv, gsend, grecv, wsend, wrecv, fsend, frecv):
+                  sbsend, sbrecv, xysend, xyrecv, abxsend, abxrecv, abysend, abyrecv, zsend, zrecv, gsend, grecv, wsend, wrecv, fsend, frecv):
     y, z, c, x = place()
     seq = lax.axis_index("seq")
     me = 2 * z + c
@@ -349,15 +349,16 @@
     handle(1, 3)
     lax.fori_loop(0, 7, ring, 0)
 
-    for yq in range(4):
+    backs = []
+    for d in (2, 1, 3, 0):
+        yq = (y + d) % 4
         out = acc[yq] / total[yq]
         for g in range(4):
             osend[yq, :, pl.ds(128 * g, 128)] = out[:, 128 * g:128 * g + 128].T.astype(BF16)
-    backs = []
-    for d in (2, 1, 3):
-        copy = remote(osend.at[(y + d) % 4], att.at[y], asend.at[d], arecv.at[d], ymates[d - 1])
-        copy.start()
-        backs.append(copy)
+        if d > 0:
+            copy = remote(osend.at[yq], att.at[y], asend.at[d], arecv.at[d], ymates[d - 1])
+            copy.start()
+            backs.append(copy)
     for yq in range(4):
         row_out[yq] = dot(picks[yq], osend[yq]).astype(BF16)
         copy = remote(row_out.at[yq], row_in.at[y], rsend.at[yq], rrecv.at[y], followers[yq])
@@ -425,23 +426,51 @@
         copy.start()
         sib_copies.append(copy)
     xy_copies = []
+    first_y, first_x = {}, {}
     for i, d in enumerate((2, 1, 3, 0)):
         mine = dot(dec[c, (y + d) % 4], grad_ref[...])
         sib_copies[i].wait_recv()
         mine = mine + sib_in[i].astype(F32)
         for j in range(4):
-            xy_out[d, j] = mine[:, 256 * j:256 * j + 256].astype(BF16)
-        for e in (2, 1, 3, 0):
-            if d == 0 and e == 0:
-                continue
-            peer = dev((y + d) % 4, z, c, (x + e) % 4)
-            copy = remote(xy_out.at[d, (x + e) % 4], xy_in.at[4 * d + e], xysend.at[4 * d + e], xyrecv.at[4 * d + e], peer)
+            a_out[d, j] = mine[:, 256 * j:256 * j + 128].astype(BF16)
+            b_out[d, j] = mine[:, 256 * j + 128:256 * j + 256].astype(BF16)
+        if d > 0:
+            copy = remote(a_out.at[d], a_in.at[d], xysend.at[d], xyrecv.at[d], ymates[d - 1])
             copy.start()
-            xy_copies.append((4 * d + e, copy))
-    mine = xy_out[0, x].astype(F32)
-    for i, copy in sorted(xy_copies, key=lambda pair: pair[0]):
-        copy.wait_recv()
-        mine = mine + xy_in[i].astype(F32)
+            first_y[d] = copy
+        for e in (2, 1, 3):
+            copy = remote(b_out.at[d, (x + e) % 4], b_in.at[e, d], xysend.at[4 * e + d], xyrecv.at[4 * e + d], xmates[e - 1])
+            copy.start()
+            first_x[e, d] = copy
+    for d in (1, 3, 2):
+        first_y[d].wait_recv()
+    for j in range(4):
+        a_two[j] = (a_out[0, j].astype(F32) + a_in[1, j].astype(F32) + a_in[2, j].astype(F32) + a_in[3, j].astype(F32)).astype(BF16)
+    second_x, second_y = {}, {}
+    for e in (2, 1, 3):
+        copy = remote(a_two.at[(x + e) % 4], a_last.at[e], abxsend.at[e], abxrecv.at[e], xmates[e - 1])
+        copy.start()
+        second_x[e] = copy
+    for d in (2, 1, 3, 0):
+        piece = b_out[d, x].astype(F32)
+        for e in (1, 2, 3):
+            first_x[e, d].wait_recv()
+            piece = piece + b_in[e, d].astype(F32)
+        b_two[d] = piece.astype(BF16)
+        if d > 0:
+            copy = remote(b_two.at[d], b_last.at[d], abysend.at[d], abyrecv.at[d], ymates[d - 1])
+            copy.start()
+            second_y[d] = copy
+    left_half = a_two[x].astype(F32)
+    for e in (1, 2, 3):
+        second_x[e].wait_recv()
+        left_half = left_half + a_last[e].astype(F32)
+    right_half = b_two[0].astype(F32)
+    for d in (1, 2, 3):
+        second_y[d].wait_recv()
+        right_half = right_half + b_last[d].astype(F32)
+    mine = jnp.concatenate([left_half, right_half], axis=1)
+    xy_copies = [(0, copy) for group_of in (first_y, first_x, second_x, second_y) for copy in group_of.values()]
     z_out[...] = mine.astype(BF16).reshape(8, 16, 256)
     z_copies = []
     for d in (4, 3, 5, 2, 6, 1, 7):
@@ -467,17 +496,10 @@
     def _():
         wcopies[0].wait_recv()
 
-    for d in (1, 3, 2):
-        there = (x + 4 - d) % 4
-        remote(xs.at[there], xs.at[there], gsend.at[d], grecv.at[d], xmates[d - 1]).wait_recv()
-
-    gains = jnp.zeros((16, 1), F32)
-    parts = jnp.zeros((1, 128), F32)
-    for j in range(4):
-        piece = xs[j]
-        gains = gains + jnp.sum(piece * wrow[:, pl.ds(256 * j, 256)].astype(F32), axis=1, keepdims=True)
-        power = jnp.sum(piece * piece, axis=0, keepdims=True)
-        parts = parts + (power[:, 0:128] + power[:, 128:256])
+    weights = wrow[:, pl.ds(pl.multiple_of(256 * x, 128), 256)].astype(F32)
+    gains = jnp.sum(piece * weights, axis=1, keepdims=True)
+    power = jnp.sum(piece * piece, axis=0, keepdims=True)
+    parts = power[:, 0:128] + power[:, 128:256]
     lane = (z % 4) * 32 + c * 16
     spread = jnp.where(iota((16, 128), 1) == iota((16, 128), 0) + lane, gains, 0.0)
     spread = jnp.sum(spread, axis=0, keepdims=True)
@@ -498,15 +520,21 @@
     tile = t1[0]
     for i in range(1, 8):
         tile = tile + t1[i]
-    t2[y] = tile
-    for d in (2, 1, 3):
-        copy = remote(t2.at[y], t2.at[y], fsend.at[7 + d], frecv.at[7 + d], ymates[d - 1])
+    t2[4 * y + x] = tile
+    for i in range(1, 16):
+        d, e = i // 4, i % 4
+        copy = remote(t2.at[4 * y + x], t2.at[4 * y + x], fsend.at[7 + i], frecv.at[7 + i], dev((y + d) % 4, z, c, (x + e) % 4))
         copy.start()
         f_copies.append(copy)
-    for d in (1, 2, 3):
-        there = (y + 4 - d) % 4
-        remote(t2.at[there], t2.at[there], fsend.at[7 + d], frecv.at[7 + d], ymates[d - 1]).wait_recv()
-    tile = (t2[0] + t2[1]) + (t2[2] + t2[3])
+    for d in (1, 3, 2):
+        there = (x + 4 - d) % 4
+        remote(xs.at[there], xs.at[there], gsend.at[d], grecv.at[d], xmates[d - 1]).wait_recv()
+    for i in range(1, 16):
+        there = 4 * ((y + 4 - i // 4) % 4) + (x + 4 - i % 4) % 4
+        remote(t2.at[there], t2.at[there], fsend.at[7 + i], frecv.at[7 + i], sibling).wait_recv()
+    tile = t2[0]
+    for i in range(1, 16):
+        tile = tile + t2[i]
     gsum = tile[0:8]
     grand = jnp.sum(tile[8:16] + gsum * gsum, axis=0, keepdims=True)
     grand = jnp.sum(grand, axis=1, keepdims=True)
@@ -570,19 +598,25 @@
             pltpu.VMEM((2, 4, 128, 512), BF16),
             pltpu.VMEM((4, 128, 1024), BF16),
             pltpu.VMEM((4, 128, 1024), BF16),
-            pltpu.VMEM((4, 4, 128, 256), BF16),
-            pltpu.VMEM((16, 128, 256), BF16),
+            pltpu.VMEM((4, 4, 128, 128), BF16),
+            pltpu.VMEM((4, 4, 128, 128), BF16),
+            pltpu.VMEM((4, 4, 128, 128), BF16),
+            pltpu.VMEM((4, 4, 128, 128), BF16),
+            pltpu.VMEM((4, 128, 128), BF16),
+            pltpu.VMEM((4, 128, 128), BF16),
+            pltpu.VMEM((4, 128, 128), BF16),
+            pltpu.VMEM((4, 128, 128), BF16),
             pltpu.VMEM((8, 16, 256), BF16),
             pltpu.VMEM((8, 16, 256), BF16),
             pltpu.VMEM((4, 16, 256), F32),
             pltpu.VMEM((16, 1024), BF16),
             pltpu.VMEM((2, 16, 128), F32),
             pltpu.VMEM((8, 16, 128), F32),
-            pltpu.VMEM((4, 16, 128), F32),
+            pltpu.VMEM((16, 16, 128), F32),
             DMA((10,)), DMA((3, 4)), DMA((3, 4)), DMA((6,)), DMA((6,)), DMA((12,)), DMA((12,)), DMA((6,)), DMA((6,)),
             DMA((8, 4)), DMA((8, 4)), DMA((16, 4)), DMA((4,)), DMA((4,)), DMA((4,)), DMA((4,)),
-            DMA((4,)), DMA((4,)), DMA((16,)), DMA((16,)), DMA((8,)), DMA((8,)), DMA((4,)), DMA((4,)),
-            DMA((3,)), DMA, DMA((11,)), DMA((11,)),
+            DMA((4,)), DMA((4,)), DMA((16,)), DMA((16,)), DMA((4,)), DMA((4,)), DMA((4,)), DMA((4,)), DMA((8,)), DMA((8,)), DMA((4,)), DMA((4,)),
+            DMA((3,)), DMA, DMA((23,)), DMA((23,)),
         ],
         compiler_params=pltpu.CompilerParams(collective_id=0, has_side_effects=True, vmem_limit_bytes=56 * 1024 * 1024),
         name="window",

time: 124 us -> 119 us (0.960)
  Pallas kernels: 123 us -> 118 us
    pallas_call x1, Pallas kernels: 122 us -> 116 us  [window(): pl.pallas_call(window_kernel, out_shape=[jax.ShapeDtypeStruct((16, 1024),...]
where the time goes in v4:
time: 119 us
  Pallas kernels  118 us (99%)
    pallas_call x1, Pallas kernels, window(): pl.pallas_call(window_kernel, out_shape=[jax.ShapeDtypeStruct((16, 1024),...  116 us

profile of v4, /device:TPU:1, one launch (start us, length us, event | category | flops | bytes accessed | tf_op | source)
XLA Modules:
  0.0 118.6 jit_solution(12217354775013448437)
XLA Ops:
  0.6 116.4 %window.1 = (f32[16,1024]{1,0:T(8,128)}, f32[8,128]{1,0:T(8,128)}) custom-call(s32[1,512]{1,0:T(1,128)} %ids_ref.1, f32[8,128]{1,0:T(8,128)} %bitcast.8, bf16[512,4096]{1,0:T(8,128)(2,1)} %bitcast.5, bf16[1024,2048]{1,0:T(8,128)(2,1)} %wq_ref.1, bf16[1024,1024]{1,0:T(8,128)(2,1)} %wkv_ref.1, bf16[512,1024]{1,0:T(8,128)(2,1)} %bitcast.6, ...), custom_call_target="tpu_custom_call" | custom-call | tf_op jit(solution)/shard_map/window/pallas_call | solution.py:572
  117.1 1.5 %finish.1 = (f32[16,1024]{1,0:T(8,128)}, f32[8,128]{1,0:T(8,128)}) custom-call(f32[16,1024]{1,0:T(8,128)} %get-tuple-element.6.rows_ref, f32[8,128]{1,0:T(8,128)} %get-tuple-element.7.gains_ref), custom_call_target="tpu_custom_call" | custom-call | tf_op jit(solution)/shard_map/finish/pallas_call | solution.py:632

commit v5 on v4

--- a/solution.py
+++ b/solution.py
@@ -91,6 +91,12 @@
         pooled[k] = chunk
         chunk = chunk.astype(F32)
         squares = squares + jnp.sum(chunk * chunk, axis=1, keepdims=True)
+    scale = lax.rsqrt(squares / 4096.0 + EPS)
+    for k in range(4):
+        chunk = pooled[k].astype(F32) * scale
+        if k == 0:
+            chunk = jnp.where((iota((PCAP, 1024), 1) == 0) & (sizes < 0.5), DEAD_ROW, chunk)
+        nrm[k, 0] = chunk.astype(BF16)
     for load in loads[4:7]:
         load.wait()
     pl.semaphore_wait(barrier, len(peers))
@@ -117,16 +123,8 @@
     for half in range(2):
         for direction in range(2):
             warrivals[direction, half ^ direction] = send_weights(direction, half ^ direction)
-    scale = lax.rsqrt(squares / 4096.0 + EPS)
     arrivals = {}
-    for k in (0, 3, 1, 2):
-        chunk = pooled[k].astype(F32) * scale
-        if k == 0:
-            chunk = jnp.where((iota((PCAP, 1024), 1) == 0) & (sizes < 0.5), DEAD_ROW, chunk)
-        nrm[k, 0] = chunk.astype(BF16)
-        direction = 0 if k < 2 else 1
-        arrivals[direction, k] = send_rows(direction, k)
-    for direction, k in ((0, 2), (1, 1), (0, 3), (1, 0)):
+    for direction, k in ((0, 0), (1, 3), (0, 1), (1, 2), (0, 2), (1, 1), (0, 3), (1, 0)):
         arrivals[direction, k] = send_rows(direction, k)
     wcopies = [remote(wout_ref.at[pl.ds(pl.multiple_of(16 * me, 16), 16)], wrow, wsend.at[d], wrecv, xmates[d]) for d in range(3)]
     wown = pltpu.make_async_copy(wout_ref.at[pl.ds(pl.multiple_of(16 * me, 16), 16)], wrow, lsem.at[9])
@@ -137,6 +135,9 @@
             copy.start()
         wown.start()
 
+    loads[7].wait()
+    for h in range(8):
+        sums_t[pl.ds(128 * h, 128)] = states_ref[:, pl.ds(128 * h, 128)].astype(F32).T
     lasts, wlasts, zgives, ssends = [], [], [], []
 
     def give(slot, side, half, i):
@@ -240,29 +241,30 @@
 
             share(2 * hop, p)
 
-    for at, step in enumerate(STEPS):
-        k = (x + step) % 4
-        value = dot(nrm[k, 0:3].reshape(384, 1024), wbuf[at])
-        if at == 0:
-            accp[0:384] = value
-        else:
-            accp[0:384] += value
+    def multiply(many, columns):
+        left = pl.ds(0, 384) if many else pl.ds(384, 128)
+        for at, step in enumerate(STEPS):
+            k = (x + step) % 4
+            chunk = nrm[k, 0:3].reshape(384, 1024) if many else nrm[k, 3]
+            value = dot(chunk, wbuf[at, :, columns])
+            if at == 0:
+                accp[left, columns] = value
+            else:
+                accp[left, columns] += value
+
+    multiply(True, pl.ds(512, 256))
     for p in range(3):
         publish(p)
+    multiply(True, pl.ds(0, 512))
     for p in range(3):
         queries(p)
     for p in range(3):
         handle(1, p)
     for copy in lasts:
         copy.wait_recv()
-    for at, step in enumerate(STEPS):
-        k = (x + step) % 4
-        value = dot(nrm[k, 3], wbuf[at])
-        if at == 0:
-            accp[384:512] = value
-        else:
-            accp[384:512] += value
+    multiply(False, pl.ds(512, 256))
     publish(3)
+    multiply(False, pl.ds(0, 512))
     queries(3)
 
     def load_keys(slots):
@@ -386,8 +388,7 @@
     scale = lax.rsqrt(squares / 2048.0 + EPS)
     for h in range(4):
         ctx_ref[h, 128:144] = (row_in[h].astype(F32) * scale).astype(BF16)
-    for load in loads[7:]:
-        load.wait()
+    loads[8].wait()
 
     own_hot = iota((144, 512), 0) == ids
     prior_hot = iota((144, 512), 0) == jnp.where(ids > 0, ids - 1, 128)
@@ -395,7 +396,7 @@
     squares = jnp.zeros((1, 512), F32)
     for h in range(8):
         lanes = pl.ds(128 * (h % 4), 128)
-        states = states_ref[:, pl.ds(128 * h, 128)].astype(F32).T
+        states = sums_t[pl.ds(128 * h, 128)]
         keys = ctx_ref[h // 4, :, lanes]
         values = ctx_ref[2 + h // 4, :, lanes]
         scores = dot(keys, states.astype(BF16)) * Q_SCALE

time: 119 us -> 117 us (0.983)
  Pallas kernels: 118 us -> 116 us
    pallas_call x1, Pallas kernels: 116 us -> 115 us  [window(): pl.pallas_call(window_kernel, out_shape=[jax.ShapeDtypeStruct((16, 1024),...]
where the time goes in v5:
time: 117 us
  Pallas kernels  116 us (99%)
    pallas_call x1, Pallas kernels, window(): pl.pallas_call(window_kernel, out_shape=[jax.ShapeDtypeStruct((16, 1024),...  115 us

profile of v5, /device:TPU:1, one launch (start us, length us, event | category | flops | bytes accessed | tf_op | source)
XLA Modules:
  0.0 116.9 jit_solution(11812113415944100121)
XLA Ops:
  0.6 114.8 %window.1 = (f32[16,1024]{1,0:T(8,128)}, f32[8,128]{1,0:T(8,128)}) custom-call(s32[1,512]{1,0:T(1,128)} %ids_ref.1, f32[8,128]{1,0:T(8,128)} %bitcast.8, bf16[512,4096]{1,0:T(8,128)(2,1)} %bitcast.5, bf16[1024,2048]{1,0:T(8,128)(2,1)} %wq_ref.1, bf16[1024,1024]{1,0:T(8,128)(2,1)} %wkv_ref.1, bf16[512,1024]{1,0:T(8,128)(2,1)} %bitcast.6, ...), custom_call_target="tpu_custom_call" | custom-call | tf_op jit(solution)/shard_map/window/pallas_call | solution.py:573
  115.5 1.5 %finish.1 = (f32[16,1024]{1,0:T(8,128)}, f32[8,128]{1,0:T(8,128)}) custom-call(f32[16,1024]{1,0:T(8,128)} %get-tuple-element.6.rows_ref, f32[8,128]{1,0:T(8,128)} %get-tuple-element.7.gains_ref), custom_call_target="tpu_custom_call" | custom-call | tf_op jit(solution)/shard_map/finish/pallas_call | solution.py:633

commit v6 on v5

--- a/solution.py
+++ b/solution.py
@@ -327,10 +327,14 @@
         hop = i // 2 + 1
         odd = 1 - i % 2
 
+        @pl.when((odd == 1) & (hop <= 3))
+        def _():
+            for p in range(3):
+                handle(hop + 1, p)
+
         @pl.when(odd == 0)
         def _():
-            for p in range(4):
-                handle(hop + 1, p)
+            handle(hop + 1, 3)
 
         mate = 7 + s + 2 * odd - s // 7
         for p in range(4):

time: 117 us -> 117 us (level)
  no operation moved by 1% of the time
where the time goes in v6:
time: 117 us
  Pallas kernels  116 us (99%)
    pallas_call x1, Pallas kernels, window(): pl.pallas_call(window_kernel, out_shape=[jax.ShapeDtypeStruct((16, 1024),...  115 us

profile of v6, /device:TPU:1, one launch (start us, length us, event | category | flops | bytes accessed | tf_op | source)
XLA Modules:
  0.0 116.9 jit_solution(4371323658352251459)
XLA Ops:
  0.6 114.7 %window.1 = (f32[16,1024]{1,0:T(8,128)}, f32[8,128]{1,0:T(8,128)}) custom-call(s32[1,512]{1,0:T(1,128)} %ids_ref.1, f32[8,128]{1,0:T(8,128)} %bitcast.8, bf16[512,4096]{1,0:T(8,128)(2,1)} %bitcast.5, bf16[1024,2048]{1,0:T(8,128)(2,1)} %wq_ref.1, bf16[1024,1024]{1,0:T(8,128)(2,1)} %wkv_ref.1, bf16[512,1024]{1,0:T(8,128)(2,1)} %bitcast.6, ...), custom_call_target="tpu_custom_call" | custom-call | tf_op jit(solution)/shard_map/window/pallas_call | solution.py:577
  115.4 1.5 %finish.1 = (f32[16,1024]{1,0:T(8,128)}, f32[8,128]{1,0:T(8,128)}) custom-call(f32[16,1024]{1,0:T(8,128)} %get-tuple-element.6.rows_ref, f32[8,128]{1,0:T(8,128)} %get-tuple-element.7.gains_ref), custom_call_target="tpu_custom_call" | custom-call | tf_op jit(solution)/shard_map/finish/pallas_call | solution.py:637
